TPU v7x, 256 devices: a whole 4x4x8 slice. The times are simulated.
256 devices in a mesh: img: 32 (over x, z), txt: 8 (over y, core).
Axes of the slice: x: 4, y: 4, z: 8, core: 2. Of those that a mesh axis runs over, the one named last changes fastest.
Arguments:
- image_emb: bfloat16 [16384, 1152], P(('img', 'txt')), may hold values from -6 to 6
- text_emb: bfloat16 [16384, 1152], P(('txt', 'img')), may hold values from -6 to 6
- log_scale: float32 [1], replicated, may hold values from 1.6 to 2.7
- bias: float32 [1], replicated, may hold values from -4 to -1
Outputs:
- loss: float32 [1], replicated
- image_grad: float32 [16384, 1152], P(('img', 'txt'))
- text_grad: float32 [16384, 1152], P(('txt', 'img'))
All inputs are finite; a program needn't handle non-finite values.
Results may differ from a plain program's by a relative error of at most 0.0007.
The roundings to bfloat16 on the way count: a program that leaves them out, or rounds other values in their place, can miss the bound.
Values may be sent and summed in bfloat16 or wider, within the bound.
A program may use at most 64 MiB of HBM per device.

v0:
```python
import jax
import jax.numpy as jnp
from jax import lax
from jax.sharding import PartitionSpec as P


def normalize(values):
    wide = values.astype(jnp.float32)
    norm = jnp.sqrt(jnp.sum(wide * wide, axis=1, keepdims=True) + 1e-06)
    direction = wide / norm
    return (norm, direction, direction.astype(jnp.bfloat16))


def project_back(dgrad, direction, norm):
    along = jnp.sum(direction * dgrad, axis=1, keepdims=True)
    return (dgrad - direction * along) / norm


def per_device(image_emb, text_emb, log_scale, bias):
    scale = jnp.exp(log_scale[0])
    offset = bias[0]
    image_norm, image_dir, image_unit = normalize(image_emb)
    text_norm, text_dir, text_unit = normalize(text_emb)
    image_rows = lax.all_gather(image_unit, "txt", axis=0, tiled=True)
    mine = lax.axis_index("img")
    row_count = image_rows.shape[0]
    row_ids = mine * row_count + jnp.arange(row_count, dtype=jnp.int32)
    text_rows = lax.all_gather(text_unit, "img", axis=0, tiled=True)
    col_count = text_rows.shape[0]
    col_ids = lax.axis_index("txt") * col_count + jnp.arange(col_count, dtype=jnp.int32)
    logits = scale * jnp.dot(image_rows, text_rows.T, preferred_element_type=jnp.float32) + offset
    label = jnp.where(row_ids[:, None] == col_ids[None, :], 1.0, -1.0).astype(jnp.float32)
    loss_part = jnp.sum(jnp.logaddexp(0.0, -label * logits))
    coef = (-label * jax.nn.sigmoid(-label * logits) * scale).astype(jnp.bfloat16)
    loss_local, coef = (loss_part, coef)
    image_part = jnp.dot(coef, text_rows, preferred_element_type=jnp.float32)
    text_dgrad = lax.psum_scatter(
        lax.dot_general(
            coef, image_rows, (((0,), (0,)), ((), ())), preferred_element_type=jnp.float32
        ),
        "img",
        scatter_dimension=0,
        tiled=True,
    )
    image_dgrad = lax.psum_scatter(image_part, "txt", scatter_dimension=0, tiled=True)
    total = image_emb.shape[0] * lax.axis_size("img") * lax.axis_size("txt")
    loss_sum = lax.psum(loss_local, ("img", "txt"))
    loss = (loss_sum / total).reshape(1)
    return (
        loss,
        project_back(image_dgrad, image_dir, image_norm),
        project_back(text_dgrad, text_dir, text_norm),
    )


def solution(mesh):
    in_specs = (P(("img", "txt"), None), P(("txt", "img"), None), P(), P())
    out_specs = (P(), P(("img", "txt"), None), P(("txt", "img"), None))
    return jax.shard_map(
        per_device, mesh=mesh, in_specs=in_specs, out_specs=out_specs, check_vma=False
    )
```

profile of v0, /device:TPU:6, one launch (start us, length us, event | category | flops | bytes accessed | tf_op | source)
XLA Modules:
  0.0 418.9 jit_solution(2614950254954094568)
XLA Ops:
  7.2 0.0 all-gather.3.cloned.1.call-start
  7.2 1.0 fusion
  8.3 1.7 fusion.2
  9.9 0.0 all-gather.3.cloned.1.call-update
  10.0 0.0 all-gather.5.cloned.1.call-start
  10.0 1.0 fusion.1
  11.1 1.7 fusion.3
  12.8 0.0 all-gather.5.cloned.1.call-update
  12.8 0.0 reduce-scatter.3.cloned.1.call-start
  14.2 25.3 %all-gather.3.cloned.1.call-done = bf16[512,1152]{1,0:T(8,128)(2,1)} async-done(((bf16[64,1152]{1,0:T(8,128)(2,1)}), bf16[512,1152]{1,0:T(8,128)(2,1)}) %all-gather.3.cloned.1.call-update) | async-done | bytes 1179664 | tf_op jit(solution)/shard_map/all_gather | solution.py:24
  39.5 84.9 %all-gather.5.cloned.1.call-done = bf16[2048,1152]{1,0:T(8,128)(2,1)} async-done(((bf16[64,1152]{1,0:T(8,128)(2,1)}), bf16[2048,1152]{1,0:T(8,128)(2,1)}) %all-gather.5.cloned.1.call-update) | async-done | bytes 4718608 | tf_op jit(solution)/shard_map/all_gather | solution.py:28
  124.5 10.0 %multiply_convert_fusion = (bf16[512,2048]{1,0:T(8,128)(2,1)S(1)}, f32[]{:T(128)}) fusion(f32[]{:T(128)} %bitcast, s32[2048]{0:T(1024)S(1)} %iota_add_fusion, s32[512]{0:T(512)S(1)} %iota_add_fusion.1, f32[]{:T(128)} %bitcast.9, bf16[512,1152]{1,0:T(8,128)(2,1)} %all-gather.3.cloned.1.call-done, bf16[2048,1152]{1,0:T(8,128)(2,1)} %all-gather.5.cloned.1.call-done), kind=kOutput, calls=%fused_computation | convolution fusion | flops 2436890624 | bytes 8005644 | tf_op jit(solution)/shard_map/dot_general | solution.py:31
  134.5 4.3 %fusion.4 = f32[512,1152]{1,0:T(8,128)} fusion(bf16[512,2048]{1,0:T(8,128)(2,1)S(1)} %get-tuple-element.3, bf16[2048,1152]{1,0:T(8,128)(2,1)S(1)} %copy-done.2), kind=kOutput, calls=%fused_computation.20 | convolution fusion | flops 2415919104 | bytes 9175040 | tf_op jit(solution)/shard_map/dot_general | solution.py:36
  138.8 0.0 reduce-scatter.3.cloned.1.call-update
  138.8 0.0 reduce-scatter.5.cloned.1.call-start
  138.8 5.3 %fusion.5 = f32[2048,1152]{1,0:T(8,128)} fusion(bf16[512,2048]{1,0:T(8,128)(2,1)S(1)} %get-tuple-element.3, bf16[512,1152]{1,0:T(8,128)(2,1)S(1)} %copy-done.3), kind=kOutput, calls=%fused_computation.21 | convolution fusion | flops 2415919104 | bytes 12713984 | tf_op jit(solution)/shard_map/dot_general | solution.py:38
  144.2 0.0 reduce-scatter.5.cloned.1.call-update
  144.2 75.2 %psum.7 = f32[]{:T(128)} all-reduce(f32[]{:T(128)} %get-tuple-element.4), channel_id=1, replica_groups=mesh['img'=32,'txt'=8] {'img','txt'}, use_global_device_ids=true, to_apply=%region_3.4 | all-reduce | flops 1 | bytes 8 | tf_op jit(solution)/shard_map/psum | solution.py:47
  220.0 0.0 reduce-scatter.3.cloned.1.call-done
  220.1 1.2 multiply_reduce_fusion.1
  221.3 1.8 subtract_divide_fusion.1
  223.1 185.2 %reduce-scatter.5.cloned.1.call-done = f32[64,1152]{1,0:T(8,128)} async-done(((f32[2048,1152]{1,0:T(8,128)}), f32[64,1152]{1,0:T(8,128)}) %reduce-scatter.5.cloned.1.call-update) | async-done | bytes 294928 | tf_op jit(solution)/shard_map/reduce_scatter | solution.py:37
  408.3 1.2 multiply_reduce_fusion
  409.4 1.8 subtract_divide_fusion
  (12 shorter events, 0.0 us)
Async XLA Ops:
  7.2 32.4 %all-gather.3.cloned.1.call-start = ((), (), s32[]{:S(2)}) async-start(), calls=%async_computation.2 | async-start | bytes 1327104 | tf_op jit(solution)/shard_map/all_gather | solution.py:24
  10.0 114.5 %all-gather.5.cloned.1.call-start = ((), (), s32[]{:S(2)}) async-start(), calls=%async_computation.3 | async-start | bytes 4866048 | tf_op jit(solution)/shard_map/all_gather | solution.py:28
  12.8 207.3 %reduce-scatter.3.cloned.1.call-start = ((), (), s32[]{:S(2)}) async-start(), calls=%async_computation.4 | async-start | bytes 2654208 | tf_op jit(solution)/shard_map/reduce_scatter | solution.py:45
  124.5 10.0 %copy-start.2 = (bf16[2048,1152]{1,0:T(8,128)(2,1)S(1)}, bf16[2048,1152]{1,0:T(8,128)(2,1)}, u32[]{:S(2)}) copy-start(bf16[2048,1152]{1,0:T(8,128)(2,1)} %all-gather.5.cloned.1.call-done) | copy-start | bytes 14155780
  134.5 4.4 %copy-start.3 = (bf16[512,1152]{1,0:T(8,128)(2,1)S(1)}, bf16[512,1152]{1,0:T(8,128)(2,1)}, u32[]{:S(2)}) copy-start(bf16[512,1152]{1,0:T(8,128)(2,1)} %all-gather.3.cloned.1.call-done) | copy-start | bytes 3538948
  138.8 269.5 %reduce-scatter.5.cloned.1.call-start = ((), (), s32[]{:S(2)}) async-start(), calls=%async_computation.5 | async-start | bytes 9732096 | tf_op jit(solution)/shard_map/reduce_scatter | solution.py:37
  144.2 75.9 %copy-start = (bf16[64,1152]{1,0:T(8,128)(2,1)S(1)}, bf16[64,1152]{1,0:T(8,128)(2,1)}, u32[]{:S(2)}) copy-start(bf16[64,1152]{1,0:T(8,128)(2,1)} %param.4) | copy-start | bytes 442372
  144.2 264.1 %copy-start.1 = (bf16[64,1152]{1,0:T(8,128)(2,1)S(1)}, bf16[64,1152]{1,0:T(8,128)(2,1)}, u32[]{:S(2)}) copy-start(bf16[64,1152]{1,0:T(8,128)(2,1)} %param.5) | copy-start | bytes 442372
Sparse Core Ops, SparseCore 0:
  10.4 29.0 all-gather.2
  42.7 81.7 all-gather.4
  138.9 36.0 reduce-scatter.2
  178.9 229.3 reduce-scatter.4
where the time goes:
time: 420 us; the launch traced here: 419 us
  waiting for transfers between devices  296 us (70%)
  blocking collectives  75.2 us (18%)
  matrix products  19.6 us (5%)
  between operations  17 us (4%)
  other arithmetic  11.4 us (3%)
    reduce_scatter x1, waiting for transfers between devices, per_device(): lax.psum_scatter(lax.dot_general(coef, image_rows, (((0,), (0,)), ((), ()...  185 us
    all_gather x1, waiting for transfers between devices, per_device(): text_rows = lax.all_gather(text_unit, 'img', axis=0, tiled=True)  84.9 us
    psum x1, blocking collectives, per_device(): loss_sum = lax.psum(loss_local, ('img', 'txt'))  75.2 us
    all_gather x1, waiting for transfers between devices, per_device(): image_rows = lax.all_gather(image_unit, 'txt', axis=0, tiled=True)  25.3 us
    dot_general x1, matrix products, per_device(): jnp.dot(image_rows, text_rows.T, preferred_element_type=jnp.float32)  9.99 us
  transfers between devices with their start and end apart: 4, of which 3 were waited for; matrix products, arithmetic and copies ran while one was open for 3% of the time, Pallas kernels for 0%

commit v1 on v0

v1 whole, which is shorter than its diff:
```python
import functools
import heapq

import jax
import jax.numpy as jnp
from jax import lax
from jax.experimental import pallas as pl
from jax.experimental.pallas import tpu as pltpu
from jax.sharding import PartitionSpec as P

F32 = jnp.float32
BF16 = jnp.bfloat16
MESH = pl.DeviceIdType.MESH
NT = (((1,), (1,)), ((), ()))
TN = (((0,), (0,)), ((), ()))
TOTAL = 16384
LOG2E = 1.4426950408889634
POWER = 7

ROW_US = 0.049
HOP_US = 2.0
CORE_ROW_US = 0.005
CORE_HOP_US = 1.0


def encode(v):
    v2 = v * v
    return (v2 * v2 * v2 * v).astype(BF16)


def decode(w):
    w = w.astype(F32)
    m = jnp.exp2(jnp.log2(jnp.abs(w)) * (1.0 / POWER))
    return jnp.where(w < 0.0, -m, m)


class Plan:
    def __init__(self):
        self.tasks = []
        self.sends = {}

    def send(self, event, link, rows, wire=True):
        if link == "c":
            self.sends[event] = (link, rows * CORE_ROW_US, CORE_HOP_US)
        else:
            self.sends[event] = (link, rows * ROW_US, HOP_US)
        return event

    def task(self, name, deps, cost, fn, sends=(), rank=0):
        self.tasks.append((name, tuple(deps), cost, fn, tuple(sends), rank))

    def order(self):
        done, free = {}, {}
        left = list(self.tasks)
        now, out = 0.0, []
        while left:
            best = None
            for i, (name, deps, cost, fn, sends, rank) in enumerate(left):
                if any(d not in done for d in deps):
                    continue
                ready = max([done[d] for d in deps], default=0.0)
                key = (max(ready, now), rank, ready, i)
                if best is None or key < best[0]:
                    best = (key, i)
            (start, _, _, _), i = best
            name, deps, cost, fn, sends, rank = left.pop(i)
            now = start + cost
            done[name] = now
            for event in sends:
                link, wire, hop = self.sends[event]
                begin = max(now, free.get(link, 0.0))
                free[link] = begin + wire
                done[event] = begin + wire + hop
            out.append((name, deps, fn, start))
        self.span = now
        return out


def kernel(
    img_ref, txt_ref, scale_ref, bias_ref, loss_ref, igrad_ref, tgrad_ref,
    IR, TR, CF, QI, OI, DI, TP, ZS, ZR, YS, YR, LS, LC, LX, LY, LZ, send_sem, recv_sem,
):
    img, txt = lax.axis_index("img"), lax.axis_index("txt")
    x, z, y, c = img // 8, img % 8, txt // 2, txt % 2

    def device(dx=0, dy=0, dz=0, dc=0):
        return (
            lax.rem(x + dx + 4, 4) * 8 + lax.rem(z + dz + 8, 8),
            lax.rem(y + dy + 4, 4) * 2 + lax.rem(c + dc, 2),
        )

    ways = {
        "x+": device(dx=1), "x-": device(dx=-1), "y+": device(dy=1), "y-": device(dy=-1),
        "z+": device(dz=1), "z-": device(dz=-1), "c": device(dc=1),
    }
    far = {("x", k): device(dx=k) for k in range(1, 4)}
    far |= {("y", k): device(dy=k) for k in range(1, 4)}
    far |= {("z", k): device(dz=k) for k in range(1, 8)}

    barrier = pltpu.get_barrier_semaphore()
    greeted = [ways["c"], *far.values()]
    for peer in greeted:
        pl.semaphore_signal(barrier, inc=1, device_id=peer, device_id_type=MESH)

    scale = jnp.exp(jnp.full((1, 1), scale_ref[0], F32))
    offset = jnp.full((1, 1), bias_ref[0], F32)

    def norm_of(ref):
        wide = ref[...].astype(F32)
        norm = jnp.sqrt(jnp.sum(wide * wide, axis=1, keepdims=True) + 1e-06)
        return wide, norm

    wide, norm = norm_of(img_ref)
    IR[0:64, :] = (wide / norm).astype(BF16)
    wide, norm = norm_of(txt_ref)
    TR[0:64, :] = (wide / norm).astype(BF16)
    LS[...] = jnp.zeros_like(LS)
    pl.semaphore_wait(barrier, len(greeted))

    plan = Plan()
    copies = {}

    def start(event, link, src, dst):
        peer = ways[link] if isinstance(link, str) else far[link]
        index = len(copies)
        copy = pltpu.make_async_remote_copy(
            src_ref=src, dst_ref=dst, send_sem=send_sem.at[index], recv_sem=recv_sem.at[index],
            device_id=peer, device_id_type=MESH,
        )
        copy.start()
        copies[event] = copy

    def forward(name, deps, cost, moves):
        def run():
            for event, link, ref, here, there, rows in moves:
                start(event, link, ref.at[pl.ds(here, rows)], ref.at[pl.ds(there, rows)])

        for event, link, ref, here, there, rows in moves:
            plan.send(event, link, rows)
        plan.task(name, deps, cost, run, [m[0] for m in moves], rank=-1)

    def islot(dz, p):
        return dz * 128 + p * 32

    def image_move(dz, p, way):
        to = (dz - 1) % 8 if way == "z+" else (dz + 1) % 8
        return (("I", to, p), way, IR, islot(dz, p), islot(to, p), 32)

    def tslot(dx, dy, half, q=0):
        return (dx * 4 + dy) * 64 + half * 32 + q * 16

    def text_move(dx, dy, half, way, q=None):
        ex, ey = dx, dy
        if way[0] == "x":
            ex = (dx - 1) % 4 if way == "x+" else (dx + 1) % 4
        else:
            ey = (dy - 1) % 4 if way == "y+" else (dy + 1) % 4
        rows = 32 if q is None else 16
        return (
            ("T", ex, ey, half, q), way, TR,
            tslot(dx, dy, half, q or 0), tslot(ex, ey, half, q or 0), rows,
        )

    first = [image_move(0, 0, "z+"), image_move(0, 0, "z-")]
    first += [text_move(0, 0, 0, "x+"), text_move(0, 0, 0, "x-")]
    first += [text_move(0, 0, 1, "y+"), text_move(0, 0, 1, "y-")]
    first += [text_move(0, 0, 0, "y+"), text_move(0, 0, 0, "y-")]
    first += [text_move(0, 0, 1, "x+"), text_move(0, 0, 1, "x-")]
    first += [image_move(0, 1, "z+"), image_move(0, 1, "z-")]
    first += [(("J", 0), "c", IR, 0, 64, 64)]
    forward("first", [], 0.3, first)
    for p in range(2):
        for dz in (7, 6, 5):
            if dz != 5 or p == 0:
                forward(("fI", dz, p), [("I", dz, p)], 0.05, [image_move(dz, p, "z+")])
        for dz in (1, 2, 3):
            if dz != 3 or p == 1:
                forward(("fI", dz, p), [("I", dz, p)], 0.05, [image_move(dz, p, "z-")])
    for dz in range(1, 8):
        forward(
            ("fJ", dz), [("I", dz, 0), ("I", dz, 1)], 0.05,
            [(("J", dz), "c", IR, dz * 128, dz * 128 + 64, 64)],
        )
    text_parts = {}
    for half in range(2):
        one, two = ("x", "y") if half == 0 else ("y", "x")

        def at(a, b):
            return (a, b) if half == 0 else (b, a)

        def ev(a, b, q=None):
            return ("T", *at(a, b), half, q)

        def mv(a, b, way, q=None):
            return text_move(*at(a, b), half, way, q)

        forward(
            ("f1", half, 3), [ev(3, 0)], 0.1,
            [mv(3, 0, two + "+"), mv(3, 0, two + "-"), mv(3, 0, one + "+", 0)],
        )
        forward(
            ("f1", half, 1), [ev(1, 0)], 0.1,
            [mv(1, 0, two + "+"), mv(1, 0, two + "-"), mv(1, 0, one + "-", 1)],
        )
        for q in range(2):
            forward(
                ("f1", half, 2, q), [ev(2, 0, q)], 0.1,
                [mv(2, 0, two + "+", q), mv(2, 0, two + "-", q)],
            )
        for a in (0, 3, 1):
            forward(("f2", half, a, 3), [ev(a, 3)], 0.05, [mv(a, 3, two + "+", 0)])
            forward(("f2", half, a, 1), [ev(a, 1)], 0.05, [mv(a, 1, two + "-", 1)])
        forward(("f2", half, 2, 3), [ev(2, 3, 0)], 0.05, [mv(2, 3, two + "+", 0)])
        forward(("f2", half, 2, 1), [ev(2, 1, 1)], 0.05, [mv(2, 1, two + "-", 1)])
        for a in range(4):
            for b in range(4):
                whole = not (a == 2 or b == 2)
                names = [ev(a, b)] if whole else [ev(a, b, 0), ev(a, b, 1)]
                if (a, b) == (0, 0):
                    names = []
                text_parts[(*at(a, b), half)] = names
    image_parts = {dz: [("I", dz, 0), ("I", dz, 1), ("J", dz)] for dz in range(8)}
    image_parts[0] = [("J", 0)]

    def coef_block(r0, c0):
        acc = lax.dot_general(
            IR[r0 : r0 + 256, :], TR[c0 : c0 + 256, :], NT, preferred_element_type=F32
        )
        e = jnp.exp2(acc * (scale * LOG2E) + offset * LOG2E)
        d = 1.0 + e
        r = pltpu.reciprocal(d, approx=True)
        r = r * (2.0 - d * r)
        CF[r0 : r0 + 256, c0 : c0 + 256] = ((e * scale) * r).astype(BF16)
        q = e[:, :128] * d[:, 128:] + e[:, 128:]
        q = q[:128] * (1.0 + q[128:]) + q[128:]
        u = 1.0 + q
        term = jnp.log(u) + (q - (u - 1.0)) * pltpu.reciprocal(u, approx=True)
        LS[...] += jnp.sum(term.reshape(16, 8, 128), axis=0)

    def diagonal():
        @pl.when(y == z // 2)
        def _():
            for other in range(4):
                pair = c * 4 + other
                dz = lax.rem(pair - z + 8, 8)
                core = lax.rem(z + c, 2)
                dx = lax.rem(other - x + 4, 4)
                dy = lax.rem(x - y + 4, 4)
                r0 = pl.multiple_of(dz * 128 + core * 64, 64)
                slot = dx * 4 + dy
                c0 = pl.multiple_of((slot // 2) * 128, 128)
                shift = lax.rem(slot, 2) * 64
                acc = lax.dot_general(
                    IR[pl.ds(r0, 64), :], TR[pl.ds(c0, 128), :], NT, preferred_element_type=F32
                )
                logit = acc * scale + offset
                rows = lax.broadcasted_iota(jnp.int32, (64, 128), 0)
                cols = lax.broadcasted_iota(jnp.int32, (64, 128), 1)
                same = cols == rows + shift
                e = jnp.exp(logit)
                mine = (-scale / (1.0 + e)).astype(BF16)
                block = CF[pl.ds(r0, 64), pl.ds(c0, 128)]
                CF[pl.ds(r0, 64), pl.ds(c0, 128)] = jnp.where(
                    same, mine.astype(F32), block.astype(F32)
                ).astype(BF16)
                less = jnp.where(same, logit, 0.0)
                LS[...] -= jnp.sum(less.reshape(8, 8, 128), axis=0)

    blocks = []
    for pair in (0, 3, 1, 2):
        for dx in (0, 1, 3, 2):
            deps = image_parts[2 * pair] + image_parts[2 * pair + 1]
            for dy in range(4):
                deps = deps + text_parts[dx, dy, 0] + text_parts[dx, dy, 1]
            name = ("coef", pair, dx)
            blocks.append(name)
            plan.task(
                name, ["first", *deps], 0.35,
                functools.partial(coef_block, pair * 256, dx * 256), rank=1,
            )
    plan.task("diag", blocks, 0.2, diagonal, rank=0)

    def spread(name, dep, value, box, place, links, events):
        def run():
            box[pl.ds(place, 1)] = value().reshape(1, 8, 128)
            for link, event in zip(links, events):
                start(event, link, box.at[pl.ds(place, 1)], box.at[pl.ds(place, 1)])

        for link, event in zip(links, events):
            plan.sends[event] = ("tiny", 0.0, 3.5)
        plan.task(name, dep, 0.1, run, events, rank=-1)

    spread("loss0", ["diag"], lambda: LS[...], LC, c, ["c"], [("Lc", 1)])
    dep = [("Lc", 1)]
    for name, box, before, place, span in (("x", LX, LC, x, 4), ("y", LY, LX, y, 4), ("z", LZ, LY, z, 8)):
        links = [(name, k) for k in range(1, span)]
        events = [("L" + name, k) for k in range(1, span)]
        spread("loss" + name, dep, functools.partial(lambda b: jnp.sum(b[...], axis=0), before), box, place, links, events)
        dep = events

    def loss_end():
        loss_ref[0] = jnp.sum(jnp.sum(LZ[...], axis=0)) * (1.0 / TOTAL)

    plan.task("loss", dep, 0.2, loss_end, rank=0)

    def image_group(pair):
        part = jnp.dot(
            CF[pair * 256 : pair * 256 + 256, :], TR[...], preferred_element_type=F32
        )
        for k in range(2):
            dz = 2 * pair + k
            QI[dz * 64 : dz * 64 + 64, :] = part[k * 128 : k * 128 + 64]
            OI[dz * 64 : dz * 64 + 64, :] = part[k * 128 + 64 : k * 128 + 128]
            rows = pl.ds(dz * 64, 64)
            start(("D", dz), "c", OI.at[rows], DI.at[rows])

    def text_group(dx):
        TP[dx * 256 : dx * 256 + 256, :] = lax.dot_general(
            CF[:, dx * 256 : dx * 256 + 256], IR[...], TN, preferred_element_type=F32
        )

    for dz in range(8):
        plan.send(("D", dz), "c", 128)
    for pair, dx in ((2, 2), (1, 1), (3, 3), (0, 0)):
        plan.task(
            ("G", pair), ["diag"], 0.95, functools.partial(image_group, pair),
            [("D", 2 * pair), ("D", 2 * pair + 1)], rank=1,
        )
        plan.task(("TG", dx), ["diag"], 0.95, functools.partial(text_group, dx), rank=1)

    zplace = {}

    def zbox(box, way, dz, p):
        i = zplace.setdefault((way, dz, p), len(zplace))
        return box.at[pl.ds(i * 32, 32)]

    def image_step(way, dz, p, arrived):
        rows = slice(dz * 64 + p * 32, dz * 64 + p * 32 + 32)
        v = QI[rows, :] + DI[rows, :]
        if arrived:
            before = dz + 1 if way == "z+" else dz - 1
            v = v + decode(zbox(ZR, way, before, p)[...])
        zbox(ZS, way, dz, p)[...] = encode(v)
        start(("R", way, dz, p), way, zbox(ZS, way, dz, p), zbox(ZR, way, dz, p))

    for way, places in (("z+", (4, 3, 2, 1)), ("z-", (4, 5, 6, 7))):
        for at_step, dz in enumerate(places):
            for p in range(2):
                keep = 0 if way == "z+" else 1
                if at_step == 0 and p != keep:
                    continue
                arrived = at_step > 1 or (at_step == 1 and p == keep)
                deps = [("G", dz // 2), ("D", dz)]
                if arrived:
                    deps.append(("R", way, places[at_step - 1], p))
                event = plan.send(("R", way, dz, p), way, 32)
                plan.task(
                    ("step", way, dz, p), deps, 0.12,
                    functools.partial(image_step, way, dz, p, arrived), [event], rank=-1,
                )

    def project(emb_ref, rows, dgrad, out_ref):
        wide = emb_ref[rows, :].astype(F32)
        norm = jnp.sqrt(jnp.sum(wide * wide, axis=1, keepdims=True) + 1e-06)
        direction = wide / norm
        along = jnp.sum(direction * dgrad, axis=1, keepdims=True)
        out_ref[rows, :] = (dgrad - direction * along) / norm

    def image_end(p):
        rows = slice(p * 32, p * 32 + 32)
        v = QI[rows, :] + DI[rows, :]
        v = v + decode(zbox(ZR, "z+", 1, p)[...]) + decode(zbox(ZR, "z-", 7, p)[...])
        project(img_ref, rows, v, igrad_ref)

    for p in range(2):
        plan.task(
            ("image_end", p), [("G", 0), ("D", 0), ("R", "z+", 1, p), ("R", "z-", 7, p)], 0.25,
            functools.partial(image_end, p), rank=0,
        )

    place = {}

    def ybox(box, key, rows):
        if key not in place:
            place[key] = sum(r for _, r in place.values()), rows
        return box.at[pl.ds(place[key][0], rows)]

    def put(event, way, v, rows):
        ybox(YS, event, rows)[...] = encode(v)
        start(event, way, ybox(YS, event, rows), ybox(YR, event, rows))

    def take(event, rows):
        return decode(ybox(YR, event, rows)[...])

    for half in range(2):
        one, two = ("y", "x") if half == 0 else ("x", "y")

        def rows_of(a, b, q=None, half=half):
            s = tslot(b, a, half) if half == 0 else tslot(a, b, half)
            if q is None:
                return slice(s, s + 32)
            return slice(s + 16 * q, s + 16 * q + 16)

        def group(a, b, half=half):
            return ("TG", b if half == 0 else a)

        def opening(b, half=half, one=one, rows_of=rows_of):
            put(("U", half, b, 1), one + "+", TP[rows_of(2, b, 0), :], 16)
            put(("U", half, b, 3), one + "-", TP[rows_of(2, b, 1), :], 16)

        def middle(b, a, half=half, one=one, rows_of=rows_of):
            q = 0 if a == 1 else 1
            rows = rows_of(a, b, q)
            TP[rows, :] = TP[rows, :] + take(("U", half, b, a), 16)
            way = one + ("+" if a == 1 else "-")
            put(("U", half, b, 0, a), way, TP[rows_of(a, b), :], 32)

        def joined(b, half=half, rows_of=rows_of):
            return TP[rows_of(0, b), :] + take(("U", half, b, 0, 1), 32) + take(("U", half, b, 0, 3), 32)

        def second(half=half, two=two, joined=joined):
            v = joined(2)
            put(("V", half, 1), two + "+", v[:16], 16)
            put(("V", half, 3), two + "-", v[16:], 16)

        def third(b, half=half, two=two, joined=joined, rows_of=rows_of):
            rows = rows_of(0, b)
            TP[rows, :] = joined(b)
            q = 0 if b == 1 else 1
            part = rows_of(0, b, q)
            TP[part, :] = TP[part, :] + take(("V", half, b), 16)
            way = two + ("+" if b == 1 else "-")
            put(("V", half, 0, b), way, TP[rows, :], 32)

        def end(half=half, joined=joined):
            v = joined(0) + take(("V", half, 0, 1), 32) + take(("V", half, 0, 3), 32)
            project(txt_ref, slice(half * 32, half * 32 + 32), v, tgrad_ref)

        for b in (2, 1, 3, 0):
            events = [
                plan.send(("U", half, b, 1), one + "+", 16),
                plan.send(("U", half, b, 3), one + "-", 16),
            ]
            plan.task(
                ("open", half, b), [group(2, b)], 0.1,
                functools.partial(opening, b), events, rank=-1,
            )
            for a, way in ((1, one + "+"), (3, one + "-")):
                event = plan.send(("U", half, b, 0, a), way, 32)
                plan.task(
                    ("mid", half, b, a), [group(a, b), ("U", half, b, a)], 0.15,
                    functools.partial(middle, b, a), [event], rank=-1,
                )
        base = {b: [group(0, b), ("U", half, b, 0, 1), ("U", half, b, 0, 3)] for b in range(4)}
        events = [
            plan.send(("V", half, 1), two + "+", 16),
            plan.send(("V", half, 3), two + "-", 16),
        ]
        plan.task(("second", half), base[2], 0.2, second, events, rank=-2)
        for b, way in ((1, two + "+"), (3, two + "-")):
            event = plan.send(("V", half, 0, b), way, 32)
            plan.task(
                ("third", half, b), [*base[b], ("V", half, b)], 0.25,
                functools.partial(third, b), [event], rank=-2,
            )
        plan.task(
            ("text_end", half), [*base[0], ("V", half, 0, 1), ("V", half, 0, 3)], 0.3, end, rank=0
        )

    landed = set()

    def land(event):
        if event in plan.sends and event not in landed:
            copies[event].wait_recv()
            landed.add(event)

    for name, deps, fn, _ in plan.order():
        for event in deps:
            land(event)
        fn()
    for event in copies:
        land(event)
    for copy in copies.values():
        copy.wait_send()


def per_device(image_emb, text_emb, log_scale, bias):
    width = image_emb.shape[1]
    vmem = pl.BlockSpec(memory_space=pltpu.VMEM)
    smem = pl.BlockSpec(memory_space=pltpu.SMEM)
    ring = 14 * 32
    return pl.pallas_call(
        kernel,
        out_shape=(
            jax.ShapeDtypeStruct((1,), F32),
            jax.ShapeDtypeStruct((64, width), F32),
            jax.ShapeDtypeStruct((64, width), F32),
        ),
        in_specs=[vmem, vmem, smem, smem],
        out_specs=(smem, vmem, vmem),
        scratch_shapes=[
            pltpu.VMEM((1024, width), BF16),
            pltpu.VMEM((1024, width), BF16),
            pltpu.VMEM((1024, 1024), BF16),
            pltpu.VMEM((512, width), F32),
            pltpu.VMEM((512, width), F32),
            pltpu.VMEM((512, width), F32),
            pltpu.VMEM((1024, width), F32),
            pltpu.VMEM((ring, width), BF16),
            pltpu.VMEM((ring, width), BF16),
            pltpu.VMEM((960, width), BF16),
            pltpu.VMEM((960, width), BF16),
            pltpu.VMEM((8, 128), F32),
            pltpu.VMEM((2, 8, 128), F32),
            pltpu.VMEM((4, 8, 128), F32),
            pltpu.VMEM((4, 8, 128), F32),
            pltpu.VMEM((8, 8, 128), F32),
            pltpu.SemaphoreType.DMA((160,)),
            pltpu.SemaphoreType.DMA((160,)),
        ],
        compiler_params=pltpu.CompilerParams(
            collective_id=0, has_side_effects=True, vmem_limit_bytes=56 << 20
        ),
        cost_estimate=pl.CostEstimate(
            flops=6 * 1024 * 1024 * width, bytes_accessed=64 * width * 12, transcendentals=1 << 22
        ),
    )(image_emb, text_emb, log_scale, bias)


def solution(mesh):
    in_specs = (P(("img", "txt"), None), P(("txt", "img"), None), P(), P())
    out_specs = (P(), P(("img", "txt"), None), P(("txt", "img"), None))
    return jax.shard_map(
        per_device, mesh=mesh, in_specs=in_specs, out_specs=out_specs, check_vma=False
    )
```

time: 420 us -> 65 us (0.15)
  waiting for transfers between devices: 296 us -> 0 us
  blocking collectives: 75.2 us -> 0 us
  Pallas kernels: 0 us -> 58.6 us
  matrix products: 19.6 us -> 0 us
  between operations: 17 us -> 3.75 us
  other arithmetic: 11.4 us -> 0 us
    reduce_scatter x2 -> x0, waiting for transfers between devices: 185 us -> none  [the longest x1 185 us: per_device(): lax.psum_scatter(lax.dot_general(coef, image_rows, (((0,), (0,)), ((), ()...]
    all_gather x2 -> x0, waiting for transfers between devices: 110 us -> none  [the longest x1 84.9 us: per_device(): text_rows = lax.all_gather(text_unit, 'img', axis=0, tiled=True)]
    psum x1 -> x0, blocking collectives: 75.2 us -> none  [per_device(): loss_sum = lax.psum(loss_local, ('img', 'txt'))]
    pallas_call x0 -> x1, Pallas kernels: none -> 58.6 us  [per_device(): pl.pallas_call(kernel, out_shape=(jax.ShapeDtypeStruct((1,), F32), jax.Sh...]
    dot_general x3 -> x0, matrix products: 19.6 us -> none  [the longest x1 9.99 us: per_device(): jnp.dot(image_rows, text_rows.T, preferred_element_type=jnp.float32)]
    reduce_sum x4 -> x0, other arithmetic: 4.43 us -> none  [the longest x2 2.35 us: project_back(): along = jnp.sum(direction * dgrad, axis=1, keepdims=True)]
  transfers between devices with their start and end apart: 4 -> 0, of which waited for: 3 -> 0; matrix products, arithmetic and copies ran while one was open for 3% -> 0% of each run, Pallas kernels for 0% -> 0%
where the time goes in v1:
time: 65 us; the launch traced here: 64.8 us
  Pallas kernels  58.6 us (90%)
  between operations  3.75 us (6%)
  local copies, waits for them, and re-layouts  2.46 us (4%)
    pallas_call x1, Pallas kernels, per_device(): pl.pallas_call(kernel, out_shape=(jax.ShapeDtypeStruct((1,), F32), jax.Sh...  58.6 us
    unnamed x4, local copies, waits for them, and re-layouts  2.46 us

profile of v1, /device:TPU:6, one launch (start us, length us, event | category | flops | bytes accessed | tf_op | source)
XLA Modules:
  0.0 64.8 jit_solution(17496190041387527894)
XLA Ops:
  1.9 58.6 %shard_map.67 = (f32[1]{0:T(128)}, f32[64,1152]{1,0:T(8,128)}, f32[64,1152]{1,0:T(8,128)}) custom-call(bf16[64,1152]{1,0:T(8,128)(2,1)} %img_ref.1, bf16[64,1152]{1,0:T(8,128)(2,1)} %txt_ref.1, f32[1]{0:T(128)S(6)} %copy.10.scale_ref, f32[1]{0:T(128)S(6)} %copy.11.bias_ref), custom_call_target="tpu_custom_call" | custom-call | flops 7247757312 | bytes 884736 | tf_op jit(solution)/shard_map/pallas_call | solution.py:492
  61.3 0.0 copy-start
  61.3 1.7 %copy.13 = f32[64,1152]{1,0:T(8,128)} copy(f32[64,1152]{1,0:T(8,128)} %get-tuple-element.7) | data formatting | bytes 589824
  63.0 0.0 copy-done
  63.0 0.7 %copy.14 = f32[64,1152]{1,0:T(8,128)} copy(f32[64,1152]{1,0:T(8,128)S(1)} %copy-done) | data formatting | bytes 589824
Async XLA Ops:
  61.3 1.8 %copy-start = (f32[64,1152]{1,0:T(8,128)S(1)}, f32[64,1152]{1,0:T(8,128)}, u32[]{:S(2)}) copy-start(f32[64,1152]{1,0:T(8,128)} %get-tuple-element.8) | copy-start | bytes 884740

commit v2 on v1

v2 whole, which is shorter than its diff:
```python
import functools

import jax
import jax.numpy as jnp
from jax import lax
from jax.experimental import pallas as pl
from jax.experimental.pallas import tpu as pltpu
from jax.sharding import PartitionSpec as P

F32 = jnp.float32
BF16 = jnp.bfloat16
MESH = pl.DeviceIdType.MESH
NT = (((1,), (1,)), ((), ()))
TN = (((0,), (0,)), ((), ()))
TOTAL = 16384
LOG2E = 1.4426950408889634

CHUNKS = (
    (2, 2), (2, 1), (2, 3), (1, 2),
    (3, 2), (2, 0), (0, 2), (1, 1),
    (1, 3), (3, 1), (3, 3), (1, 0),
    (3, 0), (0, 1), (0, 3), (0, 0),
)
PLACE = {chunk: i for i, chunk in enumerate(CHUNKS)}
POWER = 7

ROW_US = 0.049
HOP_US = 2.3
FAR_US = 2.7
CORE_ROW_US = 0.005
CORE_HOP_US = 1.0


def encode(v):
    v2 = v * v
    return (v2 * v2 * v2 * v).astype(BF16)


def decode(w):
    w = w.astype(F32)
    m = jnp.exp2(jnp.log2(jnp.abs(w)) * (1.0 / POWER))
    return jnp.where(w < 0.0, -m, m)


class Plan:
    def __init__(self):
        self.tasks = []
        self.sends = {}

    def send(self, event, link, rows):
        if link == "c":
            self.sends[event] = (("c",), rows * CORE_ROW_US, CORE_HOP_US)
        elif link == "tiny":
            self.sends[event] = ((), 0.0, 4.0)
        elif link[1] == "2":
            self.sends[event] = ((link[0] + "+", link[0] + "-"), rows * ROW_US, FAR_US)
        else:
            self.sends[event] = ((link,), rows * ROW_US, HOP_US)
        return event

    def task(self, name, deps, cost, fn, sends=()):
        self.tasks.append((name, tuple(deps), cost, fn, tuple(sends)))

    def levels(self):
        users, maker = {}, {}
        for i, (name, deps, _, _, sends) in enumerate(self.tasks):
            maker[name] = i
            for d in deps:
                users.setdefault(d, []).append(i)
        level = {}

        def of(i):
            if i not in level:
                name, _, cost, _, sends = self.tasks[i]
                after = [of(j) for j in users.get(name, ())]
                for e in sends:
                    _, wire, hop = self.sends[e]
                    after += [wire + hop + of(j) for j in users.get(e, ())]
                level[i] = cost + max(after, default=0.0)
            return level[i]

        return [of(i) for i in range(len(self.tasks))]

    def order(self):
        level = self.levels()
        done, free, out = {}, {}, []
        left = list(range(len(self.tasks)))
        now = 0.0
        while left:
            best = None
            for i in left:
                deps = self.tasks[i][1]
                if any(d not in done for d in deps):
                    continue
                ready = max([done[d] for d in deps], default=0.0)
                key = (max(ready, now), -level[i], i)
                if best is None or key < best:
                    best = key
            start, _, i = best
            left.remove(i)
            name, deps, cost, fn, sends = self.tasks[i]
            now = start + cost
            done[name] = now
            for event in sends:
                links, wire, hop = self.sends[event]
                begin = max([now, *(free.get(link, 0.0) for link in links)])
                for link in links:
                    free[link] = begin + wire
                done[event] = begin + wire + hop
            out.append((name, deps, fn, start))
        self.span = now
        return out


def kernel(
    img_hbm, txt_hbm, scale_ref, bias_ref, loss_ref, igrad_ref, tgrad_ref,
    IR, TR, CF, QI, OI, DI, TP, ZS, ZR, YS, YR, LS, LC, LX, LY, LZ, img_ref, txt_ref,
    send_sem, recv_sem, in_sem,
):
    img, txt = lax.axis_index("img"), lax.axis_index("txt")
    x, z, y, c = img // 8, img % 8, txt // 2, txt % 2

    def device(dx=0, dy=0, dz=0, dc=0):
        return (
            lax.rem(x + dx + 4, 4) * 8 + lax.rem(z + dz + 8, 8),
            lax.rem(y + dy + 4, 4) * 2 + lax.rem(c + dc, 2),
        )

    ways = {
        "x+": device(dx=1), "x-": device(dx=-1), "y+": device(dy=1), "y-": device(dy=-1),
        "z+": device(dz=1), "z-": device(dz=-1), "c": device(dc=1),
        "x2": device(dx=2), "y2": device(dy=2),
    }
    far = {("x", k): device(dx=k) for k in range(1, 4)}
    far |= {("y", k): device(dy=k) for k in range(1, 4)}
    far |= {("z", k): device(dz=k) for k in range(1, 8)}

    barrier = pltpu.get_barrier_semaphore()
    greeted = list(ways.values())
    for peer in greeted:
        pl.semaphore_signal(barrier, inc=1, device_id=peer, device_id_type=MESH)
    inputs = [
        pltpu.make_async_copy(img_hbm, img_ref, in_sem.at[0]),
        pltpu.make_async_copy(txt_hbm, txt_ref, in_sem.at[1]),
    ]
    for copy in inputs:
        copy.start()

    scale = jnp.exp(jnp.full((1, 1), scale_ref[0], F32))
    offset = jnp.full((1, 1), bias_ref[0], F32)

    def unit(ref):
        wide = ref[...].astype(F32)
        norm = jnp.sqrt(jnp.sum(wide * wide, axis=1, keepdims=True) + 1e-06)
        return (wide / norm).astype(BF16)

    LS[...] = jnp.zeros_like(LS)
    inputs[0].wait()
    IR[0:64, :] = unit(img_ref)
    inputs[1].wait()
    TR[960:1024, :] = unit(txt_ref)
    pl.semaphore_wait(barrier, len(greeted))

    plan = Plan()
    copies = {}

    def start(event, link, src, dst):
        peer = ways[link] if isinstance(link, str) else far[link]
        index = len(copies)
        copy = pltpu.make_async_remote_copy(
            src_ref=src, dst_ref=dst, send_sem=send_sem.at[index], recv_sem=recv_sem.at[index],
            device_id=peer, device_id_type=MESH,
        )
        copy.start()
        copies[event] = copy

    def forward(name, deps, moves):
        def run():
            for event, link, ref, here, there, rows in moves:
                start(event, link, ref.at[pl.ds(here, rows)], ref.at[pl.ds(there, rows)])

        for event, link, _, _, _, rows in moves:
            plan.send(event, link, rows)
        plan.task(name, deps, 0.02 + 0.03 * len(moves), run, [m[0] for m in moves])

    def islot(dz, p):
        return dz * 128 + p * 16

    def image_move(dz, p, way):
        to = (dz - 1) % 8 if way == "z+" else (dz + 1) % 8
        return (("I", to, p), way, IR, islot(dz, p), islot(to, p), 16)

    def tslot(dx, dy, half, q=0):
        return PLACE[dx, dy] * 64 + half * 32 + q * 16

    def text_move(dx, dy, half, way, q):
        step = {"+": -1, "-": 1, "2": 2}[way[1]]
        ex = (dx + step) % 4 if way[0] == "x" else dx
        ey = (dy + step) % 4 if way[0] == "y" else dy
        event = ("T", ex, ey, half, q)
        return (event, way, TR, tslot(dx, dy, half, q), tslot(ex, ey, half, q), 16)

    first = []
    for p in range(2):
        first += [image_move(0, p, "z+"), image_move(0, 3 - p, "z-")]
    for q in range(2):
        first += [text_move(0, 0, 0, w, q) for w in ("x+", "x-")]
        first += [text_move(0, 0, 1, w, q) for w in ("y+", "y-")]
    for p in range(2):
        first += [image_move(0, 2 + p, "z+"), image_move(0, 1 - p, "z-")]
    for q in range(2):
        first += [text_move(0, 0, 0, "x2", q), text_move(0, 0, 1, "y2", q)]
    for q in range(2):
        first += [text_move(0, 0, 0, w, q) for w in ("y+", "y-")]
        first += [text_move(0, 0, 1, w, q) for w in ("x+", "x-")]
    first += [(("J", 0), "c", IR, 0, 64, 64)]
    forward("first", [], first)
    for p in range(4):
        for dz in (7, 6, 5):
            if dz != 5 or p < 2:
                forward(("fI", dz, p), [("I", dz, p)], [image_move(dz, p, "z+")])
        for dz in (1, 2, 3):
            if dz != 3 or p >= 2:
                forward(("fI", dz, p), [("I", dz, p)], [image_move(dz, p, "z-")])
    for dz in range(1, 8):
        forward(
            ("fJ", dz), [("I", dz, p) for p in range(4)],
            [(("J", dz), "c", IR, dz * 128, dz * 128 + 64, 64)],
        )
    text_parts = {}
    for half in range(2):
        two = "y" if half == 0 else "x"

        def at(a, b, half=half):
            return (a, b) if half == 0 else (b, a)

        def mv(a, b, way, q, half=half, at=at):
            return text_move(*at(a, b), half, way, q)

        for a in range(4):
            for q in range(2):
                here = ("T", *at(a, 0), half, q)
                if a != 0:
                    forward(
                        ("f1", half, a, q), [here], [mv(a, 0, two + "+", q), mv(a, 0, two + "-", q)]
                    )
                b, way = ((3, "+"), (1, "-"))[q]
                forward(
                    ("f2", half, a, b), [("T", *at(a, b), half, q)], [mv(a, b, two + way, q)]
                )
            for b in range(4):
                names = [("T", *at(a, b), half, q) for q in range(2)]
                text_parts[(*at(a, b), half)] = names if (a, b) != (0, 0) else []
    image_parts = {dz: [*(("I", dz, p) for p in range(4)), ("J", dz)] for dz in range(8)}
    image_parts[0] = [("J", 0)]

    def coef_block(r0, c0):
        acc = lax.dot_general(
            IR[r0 : r0 + 256, :], TR[c0 : c0 + 256, :], NT, preferred_element_type=F32
        )
        e = jnp.exp2(acc * (scale * LOG2E) + offset * LOG2E)
        d = 1.0 + e
        r = pltpu.reciprocal(d, approx=True)
        r = r * (2.0 - d * r)
        CF[r0 : r0 + 256, c0 : c0 + 256] = ((e * scale) * r).astype(BF16)
        q = e[:, :128] * d[:, 128:] + e[:, 128:]
        q = q[:128] * (1.0 + q[128:]) + q[128:]
        u = 1.0 + q
        term = jnp.log(u) + (q - (u - 1.0)) * pltpu.reciprocal(u, approx=True)
        LS[...] += jnp.sum(term.reshape(16, 8, 128), axis=0)

    def diagonal(group):
        for other in range(4):
            pair = c * 4 + other
            dz = lax.rem(pair - z + 8, 8)
            core = lax.rem(z + c, 2)
            key = lax.rem(other - x + 4, 4) * 4 + lax.rem(x - y + 4, 4)
            slot = sum(jnp.where(key == i, PLACE[i // 4, i % 4], 0) for i in range(16))

            @pl.when(jnp.logical_and(y == z // 2, slot // 4 == group))
            def _(dz=dz, core=core, slot=slot):
                r0 = pl.multiple_of(dz * 128 + core * 64, 64)
                c0 = pl.multiple_of((slot // 2) * 128, 128)
                shift = lax.rem(slot, 2) * 64
                acc = lax.dot_general(
                    IR[pl.ds(r0, 64), :], TR[pl.ds(c0, 128), :], NT, preferred_element_type=F32
                )
                logit = acc * scale + offset
                rows = lax.broadcasted_iota(jnp.int32, (64, 128), 0)
                cols = lax.broadcasted_iota(jnp.int32, (64, 128), 1)
                same = cols == rows + shift
                e = jnp.exp(logit)
                mine = (-scale / (1.0 + e)).astype(BF16)
                block = CF[pl.ds(r0, 64), pl.ds(c0, 128)]
                CF[pl.ds(r0, 64), pl.ds(c0, 128)] = jnp.where(
                    same, mine.astype(F32), block.astype(F32)
                ).astype(BF16)
                less = jnp.where(same, logit, 0.0)
                LS[...] -= jnp.sum(less.reshape(8, 8, 128), axis=0)

    for pair in (0, 3, 1, 2):
        for group in (3, 2, 1, 0):
            deps = image_parts[2 * pair] + image_parts[2 * pair + 1]
            for dx, dy in CHUNKS[4 * group : 4 * group + 4]:
                deps = deps + text_parts[dx, dy, 0] + text_parts[dx, dy, 1]
            plan.task(
                ("coef", pair, group), ["first", *deps], 0.32,
                functools.partial(coef_block, pair * 256, group * 256),
            )
    for group in range(4):
        plan.task(
            ("diag", group), [("coef", pair, group) for pair in range(4)], 0.1,
            functools.partial(diagonal, group),
        )
    diagonals = [("diag", group) for group in range(4)]

    def spread(name, dep, value, box, place, links, events):
        def run():
            box[pl.ds(place, 1)] = value().reshape(1, 8, 128)
            for link, event in zip(links, events):
                start(event, link, box.at[pl.ds(place, 1)], box.at[pl.ds(place, 1)])

        for link, event in zip(links, events):
            plan.send(event, "tiny", 0)
        plan.task(name, dep, 0.1, run, events)

    spread("loss0", diagonals, lambda: LS[...], LC, c, ["c"], [("Lc", 1)])
    dep = [("Lc", 1)]
    for name, box, before, place, span in (("x", LX, LC, x, 4), ("y", LY, LX, y, 4), ("z", LZ, LY, z, 8)):
        links = [(name, k) for k in range(1, span)]
        events = [("L" + name, k) for k in range(1, span)]
        spread("loss" + name, dep, functools.partial(lambda b: jnp.sum(b[...], axis=0), before), box, place, links, events)
        dep = events

    def loss_end():
        loss_ref[0] = jnp.sum(jnp.sum(LZ[...], axis=0)) * (1.0 / TOTAL)

    plan.task("loss", dep, 0.1, loss_end)

    def image_group(pair):
        part = jnp.dot(
            CF[pair * 256 : pair * 256 + 256, :], TR[...], preferred_element_type=F32
        )
        for k in range(2):
            dz = 2 * pair + k
            QI[dz * 64 : dz * 64 + 64, :] = part[k * 128 : k * 128 + 64]
            OI[dz * 64 : dz * 64 + 64, :] = part[k * 128 + 64 : k * 128 + 128]
            rows = pl.ds(dz * 64, 64)
            start(("D", dz), "c", OI.at[rows], DI.at[rows])

    def text_group(group):
        cols = slice(group * 256, group * 256 + 256)
        TP[cols, :] = lax.dot_general(CF[:, cols], IR[...], TN, preferred_element_type=F32)

    for dz in range(8):
        plan.send(("D", dz), "c", 128)
    for pair, group in ((2, 0), (1, 1), (3, 2), (0, 3)):
        plan.task(("TG", group), [("diag", group)], 0.9, functools.partial(text_group, group))
        plan.task(
            ("G", pair), diagonals, 0.9, functools.partial(image_group, pair),
            [("D", 2 * pair), ("D", 2 * pair + 1)],
        )

    zplace = {}

    def zbox(box, way, dz, p):
        i = zplace.setdefault((way, dz, p), len(zplace))
        return box.at[pl.ds(i * 16, 16)]

    def image_step(way, dz, p, arrived):
        rows = slice(dz * 64 + p * 16, dz * 64 + p * 16 + 16)
        v = QI[rows, :] + DI[rows, :]
        if arrived:
            before = dz + 1 if way == "z+" else dz - 1
            v = v + decode(zbox(ZR, way, before, p)[...])
        zbox(ZS, way, dz, p)[...] = encode(v)
        start(("R", way, dz, p), way, zbox(ZS, way, dz, p), zbox(ZR, way, dz, p))

    for way, places, long in (("z+", (4, 3, 2, 1), (0, 1)), ("z-", (4, 5, 6, 7), (2, 3))):
        for step, dz in enumerate(places):
            for p in range(4):
                if step == 0 and p not in long:
                    continue
                arrived = step > 1 or (step == 1 and p in long)
                deps = [("G", dz // 2), ("D", dz)]
                if arrived:
                    deps.append(("R", way, places[step - 1], p))
                event = plan.send(("R", way, dz, p), way, 16)
                plan.task(
                    ("step", way, dz, p), deps, 0.08,
                    functools.partial(image_step, way, dz, p, arrived), [event],
                )

    def project(emb_ref, rows, dgrad, out_ref):
        wide = emb_ref[rows, :].astype(F32)
        norm = jnp.sqrt(jnp.sum(wide * wide, axis=1, keepdims=True) + 1e-06)
        direction = wide / norm
        along = jnp.sum(direction * dgrad, axis=1, keepdims=True)
        out_ref[rows, :] = (dgrad - direction * along) / norm

    def image_end(p):
        rows = slice(p * 16, p * 16 + 16)
        v = QI[rows, :] + DI[rows, :]
        v = v + decode(zbox(ZR, "z+", 1, p)[...]) + decode(zbox(ZR, "z-", 7, p)[...])
        project(img_ref, rows, v, igrad_ref)

    for p in range(4):
        plan.task(
            ("image_end", p), [("G", 0), ("D", 0), ("R", "z+", 1, p), ("R", "z-", 7, p)], 0.15,
            functools.partial(image_end, p),
        )

    place = {}

    def ybox(box, key, rows):
        if key not in place:
            place[key] = sum(r for _, r in place.values()), rows
        return box.at[pl.ds(place[key][0], rows)]

    def put(event, way, v, rows):
        ybox(YS, event, rows)[...] = encode(v)
        start(event, way, ybox(YS, event, rows), ybox(YR, event, rows))

    def take(event, rows):
        return decode(ybox(YR, event, rows)[...])

    for half in range(2):
        one, two = ("y", "x") if half == 0 else ("x", "y")

        def rows_of(a, b, q=None, half=half):
            s = tslot(b, a, half) if half == 0 else tslot(a, b, half)
            if q is None:
                return slice(s, s + 32)
            return slice(s + 16 * q, s + 16 * q + 16)

        def group(a, b, half=half):
            return ("TG", PLACE[(b, a) if half == 0 else (a, b)] // 4)

        def step(b, a, q, arrived, event, way, half=half, rows_of=rows_of):
            v = TP[rows_of(a, b, q), :]
            if arrived:
                v = v + take(("U", half, b, 2, q), 16)
            put(event, way, v, 16)

        def joined(b, half=half, rows_of=rows_of):
            parts = []
            for q in range(2):
                v = TP[rows_of(0, b, q), :]
                parts.append(v + take(("U", half, b, 1, q), 16) + take(("U", half, b, 3, q), 16))
            return jnp.concatenate(parts, axis=0)

        def second(b, way, half=half, joined=joined):
            put(("V", half, b), way, joined(b), 32)

        def end(half=half, joined=joined):
            v = joined(0)
            for b in (1, 2, 3):
                v = v + take(("V", half, b), 32)
            project(txt_ref, slice(half * 32, half * 32 + 32), v, tgrad_ref)

        def add(b, a, q, way, arrived, half=half, step=step, group=group):
            event = plan.send(("U", half, b, a, q), way, 16)
            deps = [group(a, b)]
            if arrived:
                deps.append(("U", half, b, 2, q))
            plan.task(
                ("step", half, b, a, q), deps, 0.08,
                functools.partial(step, b, a, q, arrived, event, way), [event],
            )

        for b in (2, 1, 3, 0):
            add(b, 2, 0, one + "+", False)
            add(b, 2, 1, one + "-", False)
            for q in range(2):
                add(b, 1, q, one + "+", q == 0)
                add(b, 3, q, one + "-", q == 1)
            base = [group(0, b), *(("U", half, b, a, q) for a in (1, 3) for q in range(2))]
            if b != 0:
                way = two + {2: "2", 1: "+", 3: "-"}[b]
                event = plan.send(("V", half, b), way, 32)
                plan.task(
                    ("second", half, b), base, 0.15, functools.partial(second, b, way), [event]
                )
            else:
                plan.task(("text_end", half), [*base, *(("V", half, k) for k in (1, 2, 3))], 0.3, end)

    landed = set()

    def land(event):
        if event in plan.sends and event not in landed:
            copies[event].wait_recv()
            landed.add(event)

    for name, deps, fn, _ in plan.order():
        for event in deps:
            land(event)
        fn()
    for event in copies:
        land(event)
    for copy in copies.values():
        copy.wait_send()


def per_device(image_emb, text_emb, log_scale, bias):
    width = image_emb.shape[1]
    vmem = pl.BlockSpec(memory_space=pltpu.VMEM)
    hbm = pl.BlockSpec(memory_space=pltpu.HBM)
    smem = pl.BlockSpec(memory_space=pltpu.SMEM)
    ring = 28 * 16
    return pl.pallas_call(
        kernel,
        out_shape=(
            jax.ShapeDtypeStruct((1,), F32),
            jax.ShapeDtypeStruct((64, width), F32),
            jax.ShapeDtypeStruct((64, width), F32),
        ),
        in_specs=[hbm, hbm, smem, smem],
        out_specs=(smem, vmem, vmem),
        scratch_shapes=[
            pltpu.VMEM((1024, width), BF16),
            pltpu.VMEM((1024, width), BF16),
            pltpu.VMEM((1024, 1024), BF16),
            pltpu.VMEM((512, width), F32),
            pltpu.VMEM((512, width), F32),
            pltpu.VMEM((512, width), F32),
            pltpu.VMEM((1024, width), F32),
            pltpu.VMEM((ring, width), BF16),
            pltpu.VMEM((ring, width), BF16),
            pltpu.VMEM((960, width), BF16),
            pltpu.VMEM((960, width), BF16),
            pltpu.VMEM((8, 128), F32),
            pltpu.VMEM((2, 8, 128), F32),
            pltpu.VMEM((4, 8, 128), F32),
            pltpu.VMEM((4, 8, 128), F32),
            pltpu.VMEM((8, 8, 128), F32),
            pltpu.VMEM((64, width), BF16),
            pltpu.VMEM((64, width), BF16),
            pltpu.SemaphoreType.DMA((208,)),
            pltpu.SemaphoreType.DMA((208,)),
            pltpu.SemaphoreType.DMA((2,)),
        ],
        compiler_params=pltpu.CompilerParams(
            collective_id=0, has_side_effects=True, vmem_limit_bytes=30 << 20
        ),
        cost_estimate=pl.CostEstimate(
            flops=6 * 1024 * 1024 * width, bytes_accessed=64 * width * 12, transcendentals=1 << 22
        ),
    )(image_emb, text_emb, log_scale, bias)


def solution(mesh):
    in_specs = (P(("img", "txt"), None), P(("txt", "img"), None), P(), P())
    out_specs = (P(), P(("img", "txt"), None), P(("txt", "img"), None))
    return jax.shard_map(
        per_device, mesh=mesh, in_specs=in_specs, out_specs=out_specs, check_vma=False
    )
```

time: 65 us -> 62.5 us (0.962)
  Pallas kernels: 58.6 us -> 55.3 us
  local copies, waits for them, and re-layouts: 2.46 us -> 3.24 us
    pallas_call x1, Pallas kernels: 58.6 us -> 55.3 us  [per_device(): pl.pallas_call(kernel, out_shape=(jax.ShapeDtypeStruct((1,), F32), jax.Sh...]
    unnamed x4 -> x6, local copies, waits for them, and re-layouts: 2.46 us -> 3.24 us
where the time goes in v2:
time: 62.5 us; the launch traced here: 62.2 us
  Pallas kernels  55.3 us (88%)
  between operations  3.7 us (6%)
  local copies, waits for them, and re-layouts  3.24 us (5%)
    pallas_call x1, Pallas kernels, per_device(): pl.pallas_call(kernel, out_shape=(jax.ShapeDtypeStruct((1,), F32), jax.Sh...  55.3 us
    unnamed x6, local copies, waits for them, and re-layouts  3.24 us

profile of v2, /device:TPU:6, one launch (start us, length us, event | category | flops | bytes accessed | tf_op | source)
XLA Modules:
  0.0 62.2 jit_solution(17162814497879307777)
XLA Ops:
  1.9 0.0 copy-start
  1.9 0.9 %copy-done = bf16[64,1152]{1,0:T(8,128)(2,1)S(1)} copy-done((bf16[64,1152]{1,0:T(8,128)(2,1)S(1)}, bf16[64,1152]{1,0:T(8,128)(2,1)}, u32[]{:S(2)}) %copy-start) | copy-done | bytes 147480
  2.8 0.0 copy-start.1
  2.8 0.9 %copy-done.1 = bf16[64,1152]{1,0:T(8,128)(2,1)S(1)} copy-done((bf16[64,1152]{1,0:T(8,128)(2,1)S(1)}, bf16[64,1152]{1,0:T(8,128)(2,1)}, u32[]{:S(2)}) %copy-start.1) | copy-done | bytes 147480
  3.7 55.3 %shard_map.67 = (f32[1]{0:T(128)}, f32[64,1152]{1,0:T(8,128)S(1)}, f32[64,1152]{1,0:T(8,128)S(1)}) custom-call(bf16[64,1152]{1,0:T(8,128)(2,1)S(1)} %copy-done, bf16[64,1152]{1,0:T(8,128)(2,1)S(1)} %copy-done.1, f32[1]{0:T(128)S(6)} %copy.10.scale_ref, f32[1]{0:T(128)S(6)} %copy.11.bias_ref), custom_call_target="tpu_custom_call" | custom-call | flops 7247757312 | bytes 884736 | tf_op jit(solution)/shard_map/pallas_call | solution.py:510
  59.7 0.7 %copy.13 = f32[64,1152]{1,0:T(8,128)} copy(f32[64,1152]{1,0:T(8,128)S(1)} %get-tuple-element.7) | data formatting | bytes 589824
  60.4 0.7 %copy.14 = f32[64,1152]{1,0:T(8,128)} copy(f32[64,1152]{1,0:T(8,128)S(1)} %get-tuple-element.8) | data formatting | bytes 589824
Async XLA Ops:
  1.9 0.9 %copy-start = (bf16[64,1152]{1,0:T(8,128)(2,1)S(1)}, bf16[64,1152]{1,0:T(8,128)(2,1)}, u32[]{:S(2)}) copy-start(bf16[64,1152]{1,0:T(8,128)(2,1)} %img_hbm.1) | copy-start | bytes 442372
  2.8 0.9 %copy-start.1 = (bf16[64,1152]{1,0:T(8,128)(2,1)S(1)}, bf16[64,1152]{1,0:T(8,128)(2,1)}, u32[]{:S(2)}) copy-start(bf16[64,1152]{1,0:T(8,128)(2,1)} %txt_hbm.1) | copy-start | bytes 442372

commit v3 on v2

--- a/solution.py
+++ b/solution.py
@@ -23,10 +23,11 @@
 )
 PLACE = {chunk: i for i, chunk in enumerate(CHUNKS)}
 POWER = 7
+RECEIVED = 131
 
 ROW_US = 0.049
-HOP_US = 2.3
-FAR_US = 2.7
+HOP_US = 3.0
+FAR_US = 3.4
 CORE_ROW_US = 0.005
 CORE_HOP_US = 1.0
 
@@ -46,6 +47,11 @@
     def __init__(self):
         self.tasks = []
         self.sends = {}
+        self.group = {}
+
+    def together(self, *events):
+        for event in events:
+            self.group[event] = events
 
     def send(self, event, link, rows):
         if link == "c":
@@ -59,7 +65,8 @@
         return event
 
     def task(self, name, deps, cost, fn, sends=()):
-        self.tasks.append((name, tuple(deps), cost, fn, tuple(sends)))
+        wide = dict.fromkeys(e for d in deps for e in self.group.get(d, (d,)))
+        self.tasks.append((name, tuple(wide), cost, fn, tuple(sends)))
 
     def levels(self):
         users, maker = {}, {}
@@ -162,22 +169,41 @@
     pl.semaphore_wait(barrier, len(greeted))
 
     plan = Plan()
-    copies = {}
-
-    def start(event, link, src, dst):
+    copies, pending, boxes = {}, {}, {}
+
+    def start(event, link, src, dst, sent):
         peer = ways[link] if isinstance(link, str) else far[link]
-        index = len(copies)
+        key = plan.group.get(event, (event,))
+        index = boxes.setdefault(key, len(boxes))
+        out = pending.setdefault(sent, [len(pending), 0])
+        out[1] += src.shape[0]
         copy = pltpu.make_async_remote_copy(
-            src_ref=src, dst_ref=dst, send_sem=send_sem.at[index], recv_sem=recv_sem.at[index],
+            src_ref=src, dst_ref=dst, send_sem=send_sem.at[out[0]], recv_sem=recv_sem.at[index],
             device_id=peer, device_id_type=MESH,
         )
         copy.start()
-        copies[event] = copy
+        copies[event] = copy, dst.shape[0]
+
+    landed = set()
+
+    def land(event):
+        key = plan.group.get(event, (event,))
+        if event not in plan.sends or key in landed:
+            return
+        landed.add(key)
+        if len(key) == 1:
+            copies[event][0].wait_recv()
+            return
+        rows = sum(copies[e][1] for e in key)
+        ref = whole[event[0]].at[pl.ds(0, rows)]
+        pltpu.make_async_copy(ref, ref, recv_sem.at[boxes[key]]).wait()
+
+    whole = {"I": IR, "J": IR, "T": TR, "R": IR, "U": IR, "V": IR, "Lx": LZ, "Ly": LZ, "Lz": LZ}
 
     def forward(name, deps, moves):
         def run():
             for event, link, ref, here, there, rows in moves:
-                start(event, link, ref.at[pl.ds(here, rows)], ref.at[pl.ds(there, rows)])
+                start(event, link, ref.at[pl.ds(here, rows)], ref.at[pl.ds(there, rows)], "I" if ref is IR else "T")
 
         for event, link, _, _, _, rows in moves:
             plan.send(event, link, rows)
@@ -199,6 +225,17 @@
         ey = (dy + step) % 4 if way[0] == "y" else dy
         event = ("T", ex, ey, half, q)
         return (event, way, TR, tslot(dx, dy, half, q), tslot(ex, ey, half, q), 16)
+
+    plan.together(*(("I", 4, p) for p in range(4)))
+    plan.together(("I", 5, 2), ("I", 5, 3))
+    plan.together(("I", 3, 0), ("I", 3, 1))
+    for dz in (0, 2, 6):
+        plan.together(("J", dz), ("J", dz + 1))
+    for half in range(2):
+        for a in range(4):
+            places = [(a, b) if half == 0 else (b, a) for b in range(4)]
+            plan.together(("T", *places[2], half, 0), ("T", *places[2], half, 1))
+            plan.together(("T", *places[1], half, 0), ("T", *places[3], half, 1))
 
     first = []
     for p in range(2):
@@ -254,22 +291,24 @@
     image_parts = {dz: [*(("I", dz, p) for p in range(4)), ("J", dz)] for dz in range(8)}
     image_parts[0] = [("J", 0)]
 
-    def coef_block(r0, c0):
+    def coef_block(r0, rows, c0, cols):
         acc = lax.dot_general(
-            IR[r0 : r0 + 256, :], TR[c0 : c0 + 256, :], NT, preferred_element_type=F32
+            IR[r0 : r0 + rows, :], TR[c0 : c0 + cols, :], NT, preferred_element_type=F32
         )
         e = jnp.exp2(acc * (scale * LOG2E) + offset * LOG2E)
         d = 1.0 + e
         r = pltpu.reciprocal(d, approx=True)
         r = r * (2.0 - d * r)
-        CF[r0 : r0 + 256, c0 : c0 + 256] = ((e * scale) * r).astype(BF16)
-        q = e[:, :128] * d[:, 128:] + e[:, 128:]
-        q = q[:128] * (1.0 + q[128:]) + q[128:]
+        CF[r0 : r0 + rows, c0 : c0 + cols] = ((e * scale) * r).astype(BF16)
+        w, h = cols // 2, rows // 2
+        q = e[:, :w] * d[:, w:] + e[:, w:]
+        q = q[:h] * (1.0 + q[h:]) + q[h:]
         u = 1.0 + q
         term = jnp.log(u) + (q - (u - 1.0)) * pltpu.reciprocal(u, approx=True)
-        LS[...] += jnp.sum(term.reshape(16, 8, 128), axis=0)
-
-    def diagonal(group):
+        term = jnp.sum(term.reshape(h // 8, 8, w), axis=0)
+        LS[...] += sum(term[:, k : k + 128] for k in range(0, w, 128))
+
+    def diagonal(part):
         for other in range(4):
             pair = c * 4 + other
             dz = lax.rem(pair - z + 8, 8)
@@ -277,7 +316,7 @@
             key = lax.rem(other - x + 4, 4) * 4 + lax.rem(x - y + 4, 4)
             slot = sum(jnp.where(key == i, PLACE[i // 4, i % 4], 0) for i in range(16))
 
-            @pl.when(jnp.logical_and(y == z // 2, slot // 4 == group))
+            @pl.when(jnp.logical_and(y == z // 2, dz // 2 == part))
             def _(dz=dz, core=core, slot=slot):
                 r0 = pl.multiple_of(dz * 128 + core * 64, 64)
                 c0 = pl.multiple_of((slot // 2) * 128, 128)
@@ -298,28 +337,42 @@
                 less = jnp.where(same, logit, 0.0)
                 LS[...] -= jnp.sum(less.reshape(8, 8, 128), axis=0)
 
-    for pair in (0, 3, 1, 2):
+    def text_ready(groups):
+        deps = ["first"]
+        for dx, dy in CHUNKS[4 * groups[0] : 4 * groups[-1] + 4]:
+            deps += text_parts[dx, dy, 0] + text_parts[dx, dy, 1]
+        return deps
+
+    for pair in (0, 3, 1):
         for group in (3, 2, 1, 0):
-            deps = image_parts[2 * pair] + image_parts[2 * pair + 1]
-            for dx, dy in CHUNKS[4 * group : 4 * group + 4]:
-                deps = deps + text_parts[dx, dy, 0] + text_parts[dx, dy, 1]
             plan.task(
-                ("coef", pair, group), ["first", *deps], 0.32,
-                functools.partial(coef_block, pair * 256, group * 256),
+                ("coef", pair, group),
+                image_parts[2 * pair] + image_parts[2 * pair + 1] + text_ready((group,)), 0.32,
+                functools.partial(coef_block, pair * 256, 256, group * 256, 256),
             )
-    for group in range(4):
         plan.task(
-            ("diag", group), [("coef", pair, group) for pair in range(4)], 0.1,
-            functools.partial(diagonal, group),
+            ("diag", pair), [("coef", pair, group) for group in range(4)], 0.1,
+            functools.partial(diagonal, pair),
         )
-    diagonals = [("diag", group) for group in range(4)]
+    for dz in (5, 4):
+        for groups in ((2, 3), (0, 1)):
+            plan.task(
+                ("coef", dz, groups), image_parts[dz] + text_ready(groups), 0.32,
+                functools.partial(coef_block, dz * 128, 128, groups[0] * 256, 512),
+            )
+    plan.task(
+        ("diag", 2), [("coef", dz, groups) for dz in (5, 4) for groups in ((2, 3), (0, 1))], 0.1,
+        functools.partial(diagonal, 2),
+    )
+    diagonals = [("diag", pair) for pair in range(4)]
 
     def spread(name, dep, value, box, place, links, events):
         def run():
             box[pl.ds(place, 1)] = value().reshape(1, 8, 128)
             for link, event in zip(links, events):
-                start(event, link, box.at[pl.ds(place, 1)], box.at[pl.ds(place, 1)])
-
+                start(event, link, box.at[pl.ds(place, 1)], box.at[pl.ds(place, 1)], name)
+
+        plan.together(*events)
         for link, event in zip(links, events):
             plan.send(event, "tiny", 0)
         plan.task(name, dep, 0.1, run, events)
@@ -346,7 +399,7 @@
             QI[dz * 64 : dz * 64 + 64, :] = part[k * 128 : k * 128 + 64]
             OI[dz * 64 : dz * 64 + 64, :] = part[k * 128 + 64 : k * 128 + 128]
             rows = pl.ds(dz * 64, 64)
-            start(("D", dz), "c", OI.at[rows], DI.at[rows])
+            start(("D", dz), "c", OI.at[rows], DI.at[rows], "D")
 
     def text_group(group):
         cols = slice(group * 256, group * 256 + 256)
@@ -355,9 +408,9 @@
     for dz in range(8):
         plan.send(("D", dz), "c", 128)
     for pair, group in ((2, 0), (1, 1), (3, 2), (0, 3)):
-        plan.task(("TG", group), [("diag", group)], 0.9, functools.partial(text_group, group))
+        plan.task(("TG", group), diagonals, 0.9, functools.partial(text_group, group))
         plan.task(
-            ("G", pair), diagonals, 0.9, functools.partial(image_group, pair),
+            ("G", pair), [("diag", pair)], 0.9, functools.partial(image_group, pair),
             [("D", 2 * pair), ("D", 2 * pair + 1)],
         )
 
@@ -374,8 +427,10 @@
             before = dz + 1 if way == "z+" else dz - 1
             v = v + decode(zbox(ZR, way, before, p)[...])
         zbox(ZS, way, dz, p)[...] = encode(v)
-        start(("R", way, dz, p), way, zbox(ZS, way, dz, p), zbox(ZR, way, dz, p))
-
+        start(("R", way, dz, p), way, zbox(ZS, way, dz, p), zbox(ZR, way, dz, p), "R")
+
+    ends = [("R", way, dz, p) for way, dz in (("z+", 1), ("z-", 7)) for p in range(4)]
+    plan.together(*ends)
     for way, places, long in (("z+", (4, 3, 2, 1), (0, 1)), ("z-", (4, 5, 6, 7), (2, 3))):
         for step, dz in enumerate(places):
             for p in range(4):
@@ -398,17 +453,14 @@
         along = jnp.sum(direction * dgrad, axis=1, keepdims=True)
         out_ref[rows, :] = (dgrad - direction * along) / norm
 
-    def image_end(p):
-        rows = slice(p * 16, p * 16 + 16)
-        v = QI[rows, :] + DI[rows, :]
-        v = v + decode(zbox(ZR, "z+", 1, p)[...]) + decode(zbox(ZR, "z-", 7, p)[...])
-        project(img_ref, rows, v, igrad_ref)
-
-    for p in range(4):
-        plan.task(
-            ("image_end", p), [("G", 0), ("D", 0), ("R", "z+", 1, p), ("R", "z-", 7, p)], 0.15,
-            functools.partial(image_end, p),
-        )
+    def image_end():
+        for p in range(4):
+            rows = slice(p * 16, p * 16 + 16)
+            v = QI[rows, :] + DI[rows, :]
+            v = v + decode(zbox(ZR, "z+", 1, p)[...]) + decode(zbox(ZR, "z-", 7, p)[...])
+            project(img_ref, rows, v, igrad_ref)
+
+    plan.task("image_end", [("G", 0), ("D", 0), *ends], 0.5, image_end)
 
     place = {}
 
@@ -419,7 +471,7 @@
 
     def put(event, way, v, rows):
         ybox(YS, event, rows)[...] = encode(v)
-        start(event, way, ybox(YS, event, rows), ybox(YR, event, rows))
+        start(event, way, ybox(YS, event, rows), ybox(YR, event, rows), "Y")
 
     def take(event, rows):
         return decode(ybox(YR, event, rows)[...])
@@ -468,7 +520,9 @@
                 functools.partial(step, b, a, q, arrived, event, way), [event],
             )
 
+        plan.together(*(("V", half, b) for b in (1, 2, 3)))
         for b in (2, 1, 3, 0):
+            plan.together(*(("U", half, b, a, q) for a in (1, 3) for q in range(2)))
             add(b, 2, 0, one + "+", False)
             add(b, 2, 1, one + "-", False)
             for q in range(2):
@@ -484,21 +538,16 @@
             else:
                 plan.task(("text_end", half), [*base, *(("V", half, k) for k in (1, 2, 3))], 0.3, end)
 
-    landed = set()
-
-    def land(event):
-        if event in plan.sends and event not in landed:
-            copies[event].wait_recv()
-            landed.add(event)
-
     for name, deps, fn, _ in plan.order():
         for event in deps:
             land(event)
         fn()
     for event in copies:
         land(event)
-    for copy in copies.values():
-        copy.wait_send()
+    sources = {"I": IR, "T": TR, "D": OI, "R": ZS, "Y": YS}
+    for sent, (index, rows) in pending.items():
+        ref = sources.get(sent, LZ).at[pl.ds(0, rows)]
+        pltpu.make_async_copy(ref, ref, send_sem.at[index]).wait()
 
 
 def per_device(image_emb, text_emb, log_scale, bias):
@@ -535,8 +584,8 @@
             pltpu.VMEM((8, 8, 128), F32),
             pltpu.VMEM((64, width), BF16),
             pltpu.VMEM((64, width), BF16),
-            pltpu.SemaphoreType.DMA((208,)),
-            pltpu.SemaphoreType.DMA((208,)),
+            pltpu.SemaphoreType.DMA((9,)),
+            pltpu.SemaphoreType.DMA((RECEIVED,)),
             pltpu.SemaphoreType.DMA((2,)),
         ],
         compiler_params=pltpu.CompilerParams(

time: 62.5 us -> 57.9 us (0.926)
  Pallas kernels: 55.3 us -> 50.5 us
    pallas_call x1, Pallas kernels: 55.3 us -> 50.5 us  [per_device(): pl.pallas_call(kernel, out_shape=(jax.ShapeDtypeStruct((1,), F32), jax.Sh...]
where the time goes in v3:
time: 57.9 us; the launch traced here: 57.5 us
  Pallas kernels  50.5 us (87%)
  between operations  3.7 us (6%)
  local copies, waits for them, and re-layouts  3.24 us (6%)
    pallas_call x1, Pallas kernels, per_device(): pl.pallas_call(kernel, out_shape=(jax.ShapeDtypeStruct((1,), F32), jax.Sh...  50.5 us
    unnamed x6, local copies, waits for them, and re-layouts  3.24 us

profile of v3, /device:TPU:6, one launch (start us, length us, event | category | flops | bytes accessed | tf_op | source)
XLA Modules:
  0.0 57.5 jit_solution(17283354749344399290)
XLA Ops:
  1.9 0.0 copy-start
  1.9 0.9 %copy-done = bf16[64,1152]{1,0:T(8,128)(2,1)S(1)} copy-done((bf16[64,1152]{1,0:T(8,128)(2,1)S(1)}, bf16[64,1152]{1,0:T(8,128)(2,1)}, u32[]{:S(2)}) %copy-start) | copy-done | bytes 147480
  2.8 0.0 copy-start.1
  2.8 0.9 %copy-done.1 = bf16[64,1152]{1,0:T(8,128)(2,1)S(1)} copy-done((bf16[64,1152]{1,0:T(8,128)(2,1)S(1)}, bf16[64,1152]{1,0:T(8,128)(2,1)}, u32[]{:S(2)}) %copy-start.1) | copy-done | bytes 147480
  3.7 50.5 %shard_map.67 = (f32[1]{0:T(128)}, f32[64,1152]{1,0:T(8,128)S(1)}, f32[64,1152]{1,0:T(8,128)S(1)}) custom-call(bf16[64,1152]{1,0:T(8,128)(2,1)S(1)} %copy-done, bf16[64,1152]{1,0:T(8,128)(2,1)S(1)} %copy-done.1, f32[1]{0:T(128)S(6)} %copy.10.scale_ref, f32[1]{0:T(128)S(6)} %copy.11.bias_ref), custom_call_target="tpu_custom_call" | custom-call | flops 7247757312 | bytes 884736 | tf_op jit(solution)/shard_map/pallas_call | solution.py:559
  54.9 0.7 %copy.13 = f32[64,1152]{1,0:T(8,128)} copy(f32[64,1152]{1,0:T(8,128)S(1)} %get-tuple-element.7) | data formatting | bytes 589824
  55.6 0.7 %copy.14 = f32[64,1152]{1,0:T(8,128)} copy(f32[64,1152]{1,0:T(8,128)S(1)} %get-tuple-element.8) | data formatting | bytes 589824
Async XLA Ops:
  1.9 0.9 %copy-start = (bf16[64,1152]{1,0:T(8,128)(2,1)S(1)}, bf16[64,1152]{1,0:T(8,128)(2,1)}, u32[]{:S(2)}) copy-start(bf16[64,1152]{1,0:T(8,128)(2,1)} %img_hbm.1) | copy-start | bytes 442372
  2.8 0.9 %copy-start.1 = (bf16[64,1152]{1,0:T(8,128)(2,1)S(1)}, bf16[64,1152]{1,0:T(8,128)(2,1)}, u32[]{:S(2)}) copy-start(bf16[64,1152]{1,0:T(8,128)(2,1)} %txt_hbm.1) | copy-start | bytes 442372

commit v4 on v3

--- a/solution.py
+++ b/solution.py
@@ -23,12 +23,16 @@
 )
 PLACE = {chunk: i for i, chunk in enumerate(CHUNKS)}
 POWER = 7
-RECEIVED = 131
+RECEIVED = 93
+DIRECT = (2,)
 
 ROW_US = 0.049
 HOP_US = 3.0
 FAR_US = 3.4
 CORE_ROW_US = 0.005
+SLACK_US = 0.0
+STEP_US = 0.12
+COEF_US = 0.25
 CORE_HOP_US = 1.0
 
 
@@ -100,12 +104,14 @@
                 if any(d not in done for d in deps):
                     continue
                 ready = max([done[d] for d in deps], default=0.0)
-                key = (max(ready, now), -level[i], i)
-                if best is None or key < best:
-                    best = key
-            start, _, i = best
+                slack = SLACK_US if self.tasks[i][2] > 0.24 else 0.0
+                key = (max(ready + slack, now), -level[i], i)
+                if best is None or key < best[0]:
+                    best = key, ready
+            (_, _, i), ready = best
             left.remove(i)
             name, deps, cost, fn, sends = self.tasks[i]
+            start = max(ready, now)
             now = start + cost
             done[name] = now
             for event in sends:
@@ -120,9 +126,9 @@
 
 
 def kernel(
-    img_hbm, txt_hbm, scale_ref, bias_ref, loss_ref, igrad_ref, tgrad_ref,
-    IR, TR, CF, QI, OI, DI, TP, ZS, ZR, YS, YR, LS, LC, LX, LY, LZ, img_ref, txt_ref,
-    send_sem, recv_sem, in_sem,
+    both_ref, scale_ref, bias_ref, loss_ref, igrad_ref, tgrad_ref,
+    IR, TR, CF, QI, OI, DI, TP, ZS, ZR, YS, YR, LS, LC, LX, LY, LZ,
+    send_sem, recv_sem,
 ):
     img, txt = lax.axis_index("img"), lax.axis_index("txt")
     x, z, y, c = img // 8, img % 8, txt // 2, txt % 2
@@ -146,13 +152,7 @@
     greeted = list(ways.values())
     for peer in greeted:
         pl.semaphore_signal(barrier, inc=1, device_id=peer, device_id_type=MESH)
-    inputs = [
-        pltpu.make_async_copy(img_hbm, img_ref, in_sem.at[0]),
-        pltpu.make_async_copy(txt_hbm, txt_ref, in_sem.at[1]),
-    ]
-    for copy in inputs:
-        copy.start()
-
+    img_ref, txt_ref = both_ref.at[pl.ds(0, 64)], both_ref.at[pl.ds(64, 64)]
     scale = jnp.exp(jnp.full((1, 1), scale_ref[0], F32))
     offset = jnp.full((1, 1), bias_ref[0], F32)
 
@@ -162,9 +162,7 @@
         return (wide / norm).astype(BF16)
 
     LS[...] = jnp.zeros_like(LS)
-    inputs[0].wait()
     IR[0:64, :] = unit(img_ref)
-    inputs[1].wait()
     TR[960:1024, :] = unit(txt_ref)
     pl.semaphore_wait(barrier, len(greeted))
 
@@ -226,7 +224,9 @@
         event = ("T", ex, ey, half, q)
         return (event, way, TR, tslot(dx, dy, half, q), tslot(ex, ey, half, q), 16)
 
-    plan.together(*(("I", 4, p) for p in range(4)))
+    plan.together(("I", 4, 0), ("I", 4, 1))
+    plan.together(("I", 4, 2), ("I", 4, 3))
+    plan.together(("J", 4, 0), ("J", 4, 1))
     plan.together(("I", 5, 2), ("I", 5, 3))
     plan.together(("I", 3, 0), ("I", 3, 1))
     for dz in (0, 2, 6):
@@ -235,7 +235,11 @@
         for a in range(4):
             places = [(a, b) if half == 0 else (b, a) for b in range(4)]
             plan.together(("T", *places[2], half, 0), ("T", *places[2], half, 1))
-            plan.together(("T", *places[1], half, 0), ("T", *places[3], half, 1))
+            if a in DIRECT:
+                plan.together(("T", *places[1], half, 0), ("T", *places[1], half, 1))
+                plan.together(("T", *places[3], half, 0), ("T", *places[3], half, 1))
+            else:
+                plan.together(("T", *places[1], half, 0), ("T", *places[3], half, 1))
 
     first = []
     for p in range(2):
@@ -252,17 +256,21 @@
         first += [text_move(0, 0, 1, w, q) for w in ("x+", "x-")]
     first += [(("J", 0), "c", IR, 0, 64, 64)]
     forward("first", [], first)
-    for p in range(4):
-        for dz in (7, 6, 5):
-            if dz != 5 or p < 2:
-                forward(("fI", dz, p), [("I", dz, p)], [image_move(dz, p, "z+")])
-        for dz in (1, 2, 3):
-            if dz != 3 or p >= 2:
-                forward(("fI", dz, p), [("I", dz, p)], [image_move(dz, p, "z-")])
-    for dz in range(1, 8):
+    for step in range(1, 4):
+        for p in range(4 if step < 3 else 2):
+            here = [("I", 8 - step, p), ("I", step, 3 - p)]
+            plan.together(*here)
+            moves = [image_move(8 - step, p, "z+"), image_move(step, 3 - p, "z-")]
+            forward(("fI", step, p), here, moves)
+    for dz in (1, 2, 3, 5, 6, 7):
         forward(
             ("fJ", dz), [("I", dz, p) for p in range(4)],
             [(("J", dz), "c", IR, dz * 128, dz * 128 + 64, 64)],
+        )
+    for k in range(2):
+        forward(
+            ("fJ", 4, k), [("I", 4, 2 * k), ("I", 4, 2 * k + 1)],
+            [(("J", 4, k), "c", IR, 512 + k * 32, 576 + k * 32, 32)],
         )
     text_parts = {}
     for half in range(2):
@@ -278,9 +286,12 @@
             for q in range(2):
                 here = ("T", *at(a, 0), half, q)
                 if a != 0:
-                    forward(
-                        ("f1", half, a, q), [here], [mv(a, 0, two + "+", q), mv(a, 0, two + "-", q)]
-                    )
+                    moves = [mv(a, 0, two + "+", q), mv(a, 0, two + "-", q)]
+                    if a in DIRECT:
+                        moves.append(mv(a, 0, two + "2", q))
+                    forward(("f1", half, a, q), [here], moves)
+                if a in DIRECT:
+                    continue
                 b, way = ((3, "+"), (1, "-"))[q]
                 forward(
                     ("f2", half, a, b), [("T", *at(a, b), half, q)], [mv(a, b, two + way, q)]
@@ -290,6 +301,7 @@
                 text_parts[(*at(a, b), half)] = names if (a, b) != (0, 0) else []
     image_parts = {dz: [*(("I", dz, p) for p in range(4)), ("J", dz)] for dz in range(8)}
     image_parts[0] = [("J", 0)]
+    image_parts[4][-1:] = [("J", 4, 0), ("J", 4, 1)]
 
     def coef_block(r0, rows, c0, cols):
         acc = lax.dot_general(
@@ -319,21 +331,17 @@
             @pl.when(jnp.logical_and(y == z // 2, dz // 2 == part))
             def _(dz=dz, core=core, slot=slot):
                 r0 = pl.multiple_of(dz * 128 + core * 64, 64)
+                t0 = pl.multiple_of(slot * 64, 64)
                 c0 = pl.multiple_of((slot // 2) * 128, 128)
                 shift = lax.rem(slot, 2) * 64
-                acc = lax.dot_general(
-                    IR[pl.ds(r0, 64), :], TR[pl.ds(c0, 128), :], NT, preferred_element_type=F32
-                )
-                logit = acc * scale + offset
+                pairs = IR[pl.ds(r0, 64), :].astype(F32) * TR[pl.ds(t0, 64), :].astype(F32)
+                logit = jnp.sum(pairs, axis=1, keepdims=True) * scale + offset
                 rows = lax.broadcasted_iota(jnp.int32, (64, 128), 0)
                 cols = lax.broadcasted_iota(jnp.int32, (64, 128), 1)
                 same = cols == rows + shift
-                e = jnp.exp(logit)
-                mine = (-scale / (1.0 + e)).astype(BF16)
-                block = CF[pl.ds(r0, 64), pl.ds(c0, 128)]
-                CF[pl.ds(r0, 64), pl.ds(c0, 128)] = jnp.where(
-                    same, mine.astype(F32), block.astype(F32)
-                ).astype(BF16)
+                mine = -scale / (1.0 + jnp.exp(logit))
+                block = CF[pl.ds(r0, 64), pl.ds(c0, 128)].astype(F32)
+                CF[pl.ds(r0, 64), pl.ds(c0, 128)] = jnp.where(same, mine, block).astype(BF16)
                 less = jnp.where(same, logit, 0.0)
                 LS[...] -= jnp.sum(less.reshape(8, 8, 128), axis=0)
 
@@ -343,27 +351,17 @@
             deps += text_parts[dx, dy, 0] + text_parts[dx, dy, 1]
         return deps
 
-    for pair in (0, 3, 1):
+    for pair in (0, 3, 1, 2):
         for group in (3, 2, 1, 0):
             plan.task(
                 ("coef", pair, group),
-                image_parts[2 * pair] + image_parts[2 * pair + 1] + text_ready((group,)), 0.32,
+                image_parts[2 * pair] + image_parts[2 * pair + 1] + text_ready((group,)), COEF_US,
                 functools.partial(coef_block, pair * 256, 256, group * 256, 256),
             )
         plan.task(
             ("diag", pair), [("coef", pair, group) for group in range(4)], 0.1,
             functools.partial(diagonal, pair),
         )
-    for dz in (5, 4):
-        for groups in ((2, 3), (0, 1)):
-            plan.task(
-                ("coef", dz, groups), image_parts[dz] + text_ready(groups), 0.32,
-                functools.partial(coef_block, dz * 128, 128, groups[0] * 256, 512),
-            )
-    plan.task(
-        ("diag", 2), [("coef", dz, groups) for dz in (5, 4) for groups in ((2, 3), (0, 1))], 0.1,
-        functools.partial(diagonal, 2),
-    )
     diagonals = [("diag", pair) for pair in range(4)]
 
     def spread(name, dep, value, box, place, links, events):
@@ -408,9 +406,9 @@
     for dz in range(8):
         plan.send(("D", dz), "c", 128)
     for pair, group in ((2, 0), (1, 1), (3, 2), (0, 3)):
-        plan.task(("TG", group), diagonals, 0.9, functools.partial(text_group, group))
+        plan.task(("TG", group), diagonals, 0.8, functools.partial(text_group, group))
         plan.task(
-            ("G", pair), [("diag", pair)], 0.9, functools.partial(image_group, pair),
+            ("G", pair), [("diag", pair)], 0.8, functools.partial(image_group, pair),
             [("D", 2 * pair), ("D", 2 * pair + 1)],
         )
 
@@ -420,31 +418,42 @@
         i = zplace.setdefault((way, dz, p), len(zplace))
         return box.at[pl.ds(i * 16, 16)]
 
-    def image_step(way, dz, p, arrived):
-        rows = slice(dz * 64 + p * 16, dz * 64 + p * 16 + 16)
-        v = QI[rows, :] + DI[rows, :]
-        if arrived:
-            before = dz + 1 if way == "z+" else dz - 1
-            v = v + decode(zbox(ZR, way, before, p)[...])
-        zbox(ZS, way, dz, p)[...] = encode(v)
-        start(("R", way, dz, p), way, zbox(ZS, way, dz, p), zbox(ZR, way, dz, p), "R")
+    def run_all(parts):
+        for work, _ in parts:
+            work()
+        for _, go in parts:
+            go()
+
+    def image_part(way, dz, p, arrived):
+        def work():
+            rows = slice(dz * 64 + p * 16, dz * 64 + p * 16 + 16)
+            v = QI[rows, :] + DI[rows, :]
+            if arrived:
+                before = dz + 1 if way == "z+" else dz - 1
+                v = v + decode(zbox(ZR, way, before, p)[...])
+            zbox(ZS, way, dz, p)[...] = encode(v)
+
+        def go():
+            start(("R", way, dz, p), way, zbox(ZS, way, dz, p), zbox(ZR, way, dz, p), "R")
+
+        return work, go
 
     ends = [("R", way, dz, p) for way, dz in (("z+", 1), ("z-", 7)) for p in range(4)]
     plan.together(*ends)
-    for way, places, long in (("z+", (4, 3, 2, 1), (0, 1)), ("z-", (4, 5, 6, 7), (2, 3))):
-        for step, dz in enumerate(places):
-            for p in range(4):
-                if step == 0 and p not in long:
-                    continue
-                arrived = step > 1 or (step == 1 and p in long)
-                deps = [("G", dz // 2), ("D", dz)]
-                if arrived:
-                    deps.append(("R", way, places[step - 1], p))
-                event = plan.send(("R", way, dz, p), way, 16)
-                plan.task(
-                    ("step", way, dz, p), deps, 0.08,
-                    functools.partial(image_step, way, dz, p, arrived), [event],
-                )
+    for step in range(4):
+        for p in range(4):
+            if step == 0 and p > 1:
+                continue
+            arrived = step > 1 or (step == 1 and p < 2)
+            near, away = ("z+", 4 - step, p), ("z-", 4 + step, 3 - p)
+            deps = [("G", near[1] // 2), ("D", near[1]), ("G", away[1] // 2), ("D", away[1])]
+            if arrived:
+                deps += [("R", "z+", 5 - step, p), ("R", "z-", 3 + step, 3 - p)]
+            events = [plan.send(("R", *near), "z+", 16), plan.send(("R", *away), "z-", 16)]
+            if step < 3:
+                plan.together(*events)
+            parts = [image_part(*near, arrived), image_part(*away, arrived)]
+            plan.task(("step", step, p), deps, STEP_US, functools.partial(run_all, parts), events)
 
     def project(emb_ref, rows, dgrad, out_ref):
         wide = emb_ref[rows, :].astype(F32)
@@ -469,74 +478,88 @@
             place[key] = sum(r for _, r in place.values()), rows
         return box.at[pl.ds(place[key][0], rows)]
 
-    def put(event, way, v, rows):
-        ybox(YS, event, rows)[...] = encode(v)
-        start(event, way, ybox(YS, event, rows), ybox(YR, event, rows), "Y")
-
     def take(event, rows):
         return decode(ybox(YR, event, rows)[...])
 
-    for half in range(2):
-        one, two = ("y", "x") if half == 0 else ("x", "y")
-
-        def rows_of(a, b, q=None, half=half):
-            s = tslot(b, a, half) if half == 0 else tslot(a, b, half)
-            if q is None:
-                return slice(s, s + 32)
-            return slice(s + 16 * q, s + 16 * q + 16)
-
-        def group(a, b, half=half):
-            return ("TG", PLACE[(b, a) if half == 0 else (a, b)] // 4)
-
-        def step(b, a, q, arrived, event, way, half=half, rows_of=rows_of):
-            v = TP[rows_of(a, b, q), :]
+    def rows_of(half, a, b, q=None):
+        start_row = tslot(b, a, half) if half == 0 else tslot(a, b, half)
+        if q is None:
+            return slice(start_row, start_row + 32)
+        return slice(start_row + 16 * q, start_row + 16 * q + 16)
+
+    def group(half, a, b):
+        return ("TG", PLACE[(b, a) if half == 0 else (a, b)] // 4)
+
+    def text_part(half, b, a, q, way, arrived):
+        event = ("U", half, b, a, q)
+
+        def work():
+            v = TP[rows_of(half, a, b, q), :]
             if arrived:
                 v = v + take(("U", half, b, 2, q), 16)
-            put(event, way, v, 16)
-
-        def joined(b, half=half, rows_of=rows_of):
-            parts = []
-            for q in range(2):
-                v = TP[rows_of(0, b, q), :]
-                parts.append(v + take(("U", half, b, 1, q), 16) + take(("U", half, b, 3, q), 16))
-            return jnp.concatenate(parts, axis=0)
-
-        def second(b, way, half=half, joined=joined):
-            put(("V", half, b), way, joined(b), 32)
-
-        def end(half=half, joined=joined):
-            v = joined(0)
+            ybox(YS, event, 16)[...] = encode(v)
+
+        def go():
+            start(event, way, ybox(YS, event, 16), ybox(YR, event, 16), "Y")
+
+        return work, go
+
+    def joined(half, b):
+        parts = []
+        for q in range(2):
+            v = TP[rows_of(half, 0, b, q), :]
+            for a in (1, 3):
+                v = v + take(("U", half, b, a, q), 16)
+            parts.append(v)
+        return jnp.concatenate(parts, axis=0)
+
+    def second_part(half, b, way):
+        event = ("V", half, b)
+
+        def work():
+            ybox(YS, event, 32)[...] = encode(joined(half, b))
+
+        def go():
+            start(event, way, ybox(YS, event, 32), ybox(YR, event, 32), "Y")
+
+        return work, go
+
+    def text_end():
+        for half in range(2):
+            v = joined(half, 0)
             for b in (1, 2, 3):
                 v = v + take(("V", half, b), 32)
             project(txt_ref, slice(half * 32, half * 32 + 32), v, tgrad_ref)
 
-        def add(b, a, q, way, arrived, half=half, step=step, group=group):
-            event = plan.send(("U", half, b, a, q), way, 16)
-            deps = [group(a, b)]
-            if arrived:
-                deps.append(("U", half, b, 2, q))
-            plan.task(
-                ("step", half, b, a, q), deps, 0.08,
-                functools.partial(step, b, a, q, arrived, event, way), [event],
-            )
-
-        plan.together(*(("V", half, b) for b in (1, 2, 3)))
-        for b in (2, 1, 3, 0):
-            plan.together(*(("U", half, b, a, q) for a in (1, 3) for q in range(2)))
-            add(b, 2, 0, one + "+", False)
-            add(b, 2, 1, one + "-", False)
-            for q in range(2):
-                add(b, 1, q, one + "+", q == 0)
-                add(b, 3, q, one + "-", q == 1)
-            base = [group(0, b), *(("U", half, b, a, q) for a in (1, 3) for q in range(2))]
-            if b != 0:
-                way = two + {2: "2", 1: "+", 3: "-"}[b]
-                event = plan.send(("V", half, b), way, 32)
-                plan.task(
-                    ("second", half, b), base, 0.15, functools.partial(second, b, way), [event]
-                )
-            else:
-                plan.task(("text_end", half), [*base, *(("V", half, k) for k in (1, 2, 3))], 0.3, end)
+    one, two = ("y", "x"), ("x", "y")
+    sides = ((1, "+"), (3, "-"))
+    plan.together(*(("V", half, b) for half in range(2) for b in (1, 2, 3)))
+    for b in (2, 1, 3, 0):
+        outer, fresh, passed = [], [], []
+        for half in range(2):
+            for q, (a, sign) in enumerate(sides):
+                outer.append((half, b, 2, q, one[half] + sign, False))
+                fresh.append((half, b, a, 1 - q, one[half] + sign, False))
+                passed.append((half, b, a, q, one[half] + sign, True))
+        plan.together(*(("U", *part[:4]) for part in outer))
+        plan.together(*(("U", *part[:4]) for part in fresh + passed))
+        for kind, parts in (("outer", outer), ("fresh", fresh), ("passed", passed)):
+            events = [plan.send(("U", *part[:4]), part[4], 16) for part in parts]
+            deps = [group(part[0], part[2], b) for part in parts]
+            if kind == "passed":
+                deps += [("U", half, b, 2, q) for half in range(2) for q in range(2)]
+            run = functools.partial(run_all, [text_part(*part) for part in parts])
+            plan.task((kind, b), deps, 2 * STEP_US, run, events)
+        base = [group(half, 0, b) for half in range(2)]
+        base += [("U", *part[:4]) for part in fresh + passed]
+        if b != 0:
+            ways_two = [two[half] + {2: "2", 1: "+", 3: "-"}[b] for half in range(2)]
+            events = [plan.send(("V", half, b), ways_two[half], 32) for half in range(2)]
+            parts = [second_part(half, b, ways_two[half]) for half in range(2)]
+            plan.task(("second", b), base, 0.25, functools.partial(run_all, parts), events)
+        else:
+            last = [("V", half, k) for half in range(2) for k in (1, 2, 3)]
+            plan.task("text_end", [*base, *last], 0.5, text_end)
 
     for name, deps, fn, _ in plan.order():
         for event in deps:
@@ -545,6 +568,7 @@
     for event in copies:
         land(event)
     sources = {"I": IR, "T": TR, "D": OI, "R": ZS, "Y": YS}
+    assert len(boxes) == RECEIVED
     for sent, (index, rows) in pending.items():
         ref = sources.get(sent, LZ).at[pl.ds(0, rows)]
         pltpu.make_async_copy(ref, ref, send_sem.at[index]).wait()
@@ -553,7 +577,6 @@
 def per_device(image_emb, text_emb, log_scale, bias):
     width = image_emb.shape[1]
     vmem = pl.BlockSpec(memory_space=pltpu.VMEM)
-    hbm = pl.BlockSpec(memory_space=pltpu.HBM)
     smem = pl.BlockSpec(memory_space=pltpu.SMEM)
     ring = 28 * 16
     return pl.pallas_call(
@@ -563,7 +586,7 @@
             jax.ShapeDtypeStruct((64, width), F32),
             jax.ShapeDtypeStruct((64, width), F32),
         ),
-        in_specs=[hbm, hbm, smem, smem],
+        in_specs=[vmem, smem, smem],
         out_specs=(smem, vmem, vmem),
         scratch_shapes=[
             pltpu.VMEM((1024, width), BF16),
@@ -582,11 +605,8 @@
             pltpu.VMEM((4, 8, 128), F32),
             pltpu.VMEM((4, 8, 128), F32),
             pltpu.VMEM((8, 8, 128), F32),
-            pltpu.VMEM((64, width), BF16),
-            pltpu.VMEM((64, width), BF16),
             pltpu.SemaphoreType.DMA((9,)),
             pltpu.SemaphoreType.DMA((RECEIVED,)),
-            pltpu.SemaphoreType.DMA((2,)),
         ],
         compiler_params=pltpu.CompilerParams(
             collective_id=0, has_side_effects=True, vmem_limit_bytes=30 << 20
@@ -594,7 +614,7 @@
         cost_estimate=pl.CostEstimate(
             flops=6 * 1024 * 1024 * width, bytes_accessed=64 * width * 12, transcendentals=1 << 22
         ),
-    )(image_emb, text_emb, log_scale, bias)
+    )(jnp.concatenate([image_emb, text_emb], axis=0), log_scale, bias)
 
 
 def solution(mesh):

time: 57.9 us -> 56.8 us (0.981)
  local copies, waits for them, and re-layouts: 3.24 us -> 1.43 us
  other arithmetic: 0 us -> 1.01 us
  Pallas kernels: 50.5 us -> 49.9 us
    unnamed x6 -> x2, local copies, waits for them, and re-layouts: 3.24 us -> 1.43 us
    concatenate x0 -> x1, other arithmetic: none -> 1.01 us  [per_device(): jnp.concatenate([image_emb, text_emb], axis=0)]
where the time goes in v4:
time: 56.8 us; the launch traced here: 56 us
  Pallas kernels  49.9 us (88%)
  between operations  3.62 us (6%)
  local copies, waits for them, and re-layouts  1.43 us (3%)
  other arithmetic  1.01 us (2%)
    pallas_call x1, Pallas kernels, per_device(): pl.pallas_call(kernel, out_shape=(jax.ShapeDtypeStruct((1,), F32), jax.Sh...  49.9 us
    unnamed x2, local copies, waits for them, and re-layouts  1.43 us

profile of v4, /device:TPU:6, one launch (start us, length us, event | category | flops | bytes accessed | tf_op | source)
XLA Modules:
  0.0 56.0 jit_solution(8698249187680930176)
XLA Ops:
  1.9 1.0 %pad_maximum_fusion.both_ref = bf16[128,1152]{1,0:T(8,128)(2,1)S(1)} fusion(bf16[64,1152]{1,0:T(8,128)(2,1)} %param.5, bf16[64,1152]{1,0:T(8,128)(2,1)} %param.4), kind=kLoop, calls=%fused_computation | loop fusion | flops 589824 | bytes 589824 | tf_op jit(solution)/shard_map/concatenate | solution.py:617
  2.9 49.9 %shard_map.67 = (f32[1]{0:T(128)}, f32[64,1152]{1,0:T(8,128)S(1)}, f32[64,1152]{1,0:T(8,128)S(1)}) custom-call(bf16[128,1152]{1,0:T(8,128)(2,1)S(1)} %pad_maximum_fusion.both_ref, f32[1]{0:T(128)S(6)} %copy.10.scale_ref, f32[1]{0:T(128)S(6)} %copy.11.bias_ref), custom_call_target="tpu_custom_call" | custom-call | flops 7247757312 | bytes 884736 | tf_op jit(solution)/shard_map/pallas_call | solution.py:582
  53.4 0.7 %copy.13 = f32[64,1152]{1,0:T(8,128)} copy(f32[64,1152]{1,0:T(8,128)S(1)} %get-tuple-element.7) | data formatting | bytes 589824
  54.2 0.7 %copy.14 = f32[64,1152]{1,0:T(8,128)} copy(f32[64,1152]{1,0:T(8,128)S(1)} %get-tuple-element.8) | data formatting | bytes 589824

commit v5 on v4

--- a/solution.py
+++ b/solution.py
@@ -23,16 +23,16 @@
 )
 PLACE = {chunk: i for i, chunk in enumerate(CHUNKS)}
 POWER = 7
-RECEIVED = 93
-DIRECT = (2,)
+RECEIVED = 95
+DIRECT = ()
 
 ROW_US = 0.049
 HOP_US = 3.0
 FAR_US = 3.4
 CORE_ROW_US = 0.005
 SLACK_US = 0.0
-STEP_US = 0.12
-COEF_US = 0.25
+STEP_US = 0.2
+COEF_US = 0.35
 CORE_HOP_US = 1.0
 
 
@@ -161,6 +161,14 @@
         norm = jnp.sqrt(jnp.sum(wide * wide, axis=1, keepdims=True) + 1e-06)
         return (wide / norm).astype(BF16)
 
+    fixes = []
+    for other in range(4):
+        dz = lax.rem(c * 4 + other - z + 8, 8)
+        core = lax.rem(z + c, 2)
+        key = lax.rem(other - x + 4, 4) * 4 + lax.rem(x - y + 4, 4)
+        slot = sum(jnp.where(key == i, PLACE[i // 4, i % 4], 0) for i in range(16))
+        fixes.append((dz, dz * 128 + core * 64, slot * 64, (slot // 2) * 128, lax.rem(slot, 2) * 64))
+
     LS[...] = jnp.zeros_like(LS)
     IR[0:64, :] = unit(img_ref)
     TR[960:1024, :] = unit(txt_ref)
@@ -321,29 +329,25 @@
         LS[...] += sum(term[:, k : k + 128] for k in range(0, w, 128))
 
     def diagonal(part):
-        for other in range(4):
-            pair = c * 4 + other
-            dz = lax.rem(pair - z + 8, 8)
-            core = lax.rem(z + c, 2)
-            key = lax.rem(other - x + 4, 4) * 4 + lax.rem(x - y + 4, 4)
-            slot = sum(jnp.where(key == i, PLACE[i // 4, i % 4], 0) for i in range(16))
-
-            @pl.when(jnp.logical_and(y == z // 2, dz // 2 == part))
-            def _(dz=dz, core=core, slot=slot):
-                r0 = pl.multiple_of(dz * 128 + core * 64, 64)
-                t0 = pl.multiple_of(slot * 64, 64)
-                c0 = pl.multiple_of((slot // 2) * 128, 128)
-                shift = lax.rem(slot, 2) * 64
-                pairs = IR[pl.ds(r0, 64), :].astype(F32) * TR[pl.ds(t0, 64), :].astype(F32)
-                logit = jnp.sum(pairs, axis=1, keepdims=True) * scale + offset
-                rows = lax.broadcasted_iota(jnp.int32, (64, 128), 0)
-                cols = lax.broadcasted_iota(jnp.int32, (64, 128), 1)
-                same = cols == rows + shift
-                mine = -scale / (1.0 + jnp.exp(logit))
-                block = CF[pl.ds(r0, 64), pl.ds(c0, 128)].astype(F32)
-                CF[pl.ds(r0, 64), pl.ds(c0, 128)] = jnp.where(same, mine, block).astype(BF16)
-                less = jnp.where(same, logit, 0.0)
-                LS[...] -= jnp.sum(less.reshape(8, 8, 128), axis=0)
+        @pl.when(y == z // 2)
+        def _():
+            for dz, r0, t0, c0, shift in fixes:
+
+                @pl.when(dz // 2 == part)
+                def _(r0=r0, t0=t0, c0=c0, shift=shift):
+                    r0 = pl.multiple_of(r0, 64)
+                    t0 = pl.multiple_of(t0, 64)
+                    c0 = pl.multiple_of(c0, 128)
+                    pairs = IR[pl.ds(r0, 64), :].astype(F32) * TR[pl.ds(t0, 64), :].astype(F32)
+                    logit = jnp.sum(pairs, axis=1, keepdims=True) * scale + offset
+                    rows = lax.broadcasted_iota(jnp.int32, (64, 128), 0)
+                    cols = lax.broadcasted_iota(jnp.int32, (64, 128), 1)
+                    same = cols == rows + shift
+                    mine = -scale / (1.0 + jnp.exp(logit))
+                    block = CF[pl.ds(r0, 64), pl.ds(c0, 128)].astype(F32)
+                    CF[pl.ds(r0, 64), pl.ds(c0, 128)] = jnp.where(same, mine, block).astype(BF16)
+                    less = jnp.where(same, logit, 0.0)
+                    LS[...] -= jnp.sum(less.reshape(8, 8, 128), axis=0)
 
     def text_ready(groups):
         deps = ["first"]
@@ -568,7 +572,6 @@
     for event in copies:
         land(event)
     sources = {"I": IR, "T": TR, "D": OI, "R": ZS, "Y": YS}
-    assert len(boxes) == RECEIVED
     for sent, (index, rows) in pending.items():
         ref = sources.get(sent, LZ).at[pl.ds(0, rows)]
         pltpu.make_async_copy(ref, ref, send_sem.at[index]).wait()

time: 56.8 us -> 56.3 us (level)
  Pallas kernels: 49.9 us -> 49.3 us
    pallas_call x1, Pallas kernels: 49.9 us -> 49.3 us  [per_device(): pl.pallas_call(kernel, out_shape=(jax.ShapeDtypeStruct((1,), F32), jax.Sh...]
where the time goes in v5:
time: 56.3 us; the launch traced here: 55.3 us
  Pallas kernels  49.3 us (88%)
  between operations  3.62 us (6%)
  local copies, waits for them, and re-layouts  1.43 us (3%)
  other arithmetic  1.01 us (2%)
    pallas_call x1, Pallas kernels, per_device(): pl.pallas_call(kernel, out_shape=(jax.ShapeDtypeStruct((1,), F32), jax.Sh...  49.3 us
    unnamed x2, local copies, waits for them, and re-layouts  1.43 us

profile of v5, /device:TPU:6, one launch (start us, length us, event | category | flops | bytes accessed | tf_op | source)
XLA Modules:
  0.0 55.3 jit_solution(3127060678124596725)
XLA Ops:
  1.9 1.0 %pad_maximum_fusion.both_ref = bf16[128,1152]{1,0:T(8,128)(2,1)S(1)} fusion(bf16[64,1152]{1,0:T(8,128)(2,1)} %param.5, bf16[64,1152]{1,0:T(8,128)(2,1)} %param.4), kind=kLoop, calls=%fused_computation | loop fusion | flops 589824 | bytes 589824 | tf_op jit(solution)/shard_map/concatenate | solution.py:620
  2.9 49.3 %shard_map.67 = (f32[1]{0:T(128)}, f32[64,1152]{1,0:T(8,128)S(1)}, f32[64,1152]{1,0:T(8,128)S(1)}) custom-call(bf16[128,1152]{1,0:T(8,128)(2,1)S(1)} %pad_maximum_fusion.both_ref, f32[1]{0:T(128)S(6)} %copy.10.scale_ref, f32[1]{0:T(128)S(6)} %copy.11.bias_ref), custom_call_target="tpu_custom_call" | custom-call | flops 7247757312 | bytes 884736 | tf_op jit(solution)/shard_map/pallas_call | solution.py:585
  52.8 0.7 %copy.13 = f32[64,1152]{1,0:T(8,128)} copy(f32[64,1152]{1,0:T(8,128)S(1)} %get-tuple-element.7) | data formatting | bytes 589824
  53.5 0.7 %copy.14 = f32[64,1152]{1,0:T(8,128)} copy(f32[64,1152]{1,0:T(8,128)S(1)} %get-tuple-element.8) | data formatting | bytes 589824
